TPU v7x, 256 devices: a whole 4x4x8 slice. The times are simulated.
256 devices in a mesh: dp: 16 (over y, z_hi), tp: 16 (over x, z_lo, core).
Axes of the slice: x: 4, y: 4, z: 8 (z_hi: 4, z_lo: 2; z = z_hi * 2 + z_lo), core: 2. Of those that a mesh axis runs over, the one named last changes fastest.
Arguments:
- input_rows: bfloat16 [16, 2048, 4096], P('dp', 'tp'), may hold values from -6 to 6
- queries: bfloat16 [16, 2048, 4096], P('dp', None, 'tp')
- key_values: bfloat16 [16, 2048, 1024], P('dp')
- out_grad: bfloat16 [16, 2048, 4096], P('dp', None, 'tp'), may hold values from -6 to 6
- item_logratio: float32 [16, 4], P('dp'), may hold values from -40 to 40
- pair_ids: int32 [16, 4], P('dp'), may hold values from 0 to 1, as said below
- tile_item: int32 [16, 16], P('dp'), may hold values from 0 to 3, as said below
- tile_image: int32 [16, 16], P('dp'), may hold values from 0 to 16, as said below
Outputs:
- grad_query: bfloat16 [16, 2048, 4096], P('dp', None, 'tp')
- grad_kv_weight: float32 [4096, 1024], P('dp', 'tp')
Inputs may be any that keep to these rules, and one draw needn't show every extreme that they name: Each sequence's tile_item never falls, starts at 0 and ends at 3; a response may have no tiles. `tile_image`: image tiles carry 1 plus the index of the first tile of their image; an image is a maximal run of image tiles inside one response; the last tile of a sequence is an image tile and the one before it is text. `pair_ids`: within a sequence each pair id appears for exactly two responses; the earlier of the two is the chosen response.
All inputs are finite; a program needn't handle non-finite values.
Results may differ from a plain program's by a relative error of at most 0.0065.
Values may be sent and summed in bfloat16 or wider, within the bound.
A program may use at most 128 MiB of HBM per device.

v0:
```python
import math

import jax
import jax.numpy as jnp
from jax import lax
from jax.sharding import PartitionSpec as P

KVH = 4
HD = 128
TILE = 128


BETA = 0.1
MASKED = -1e30


def from_partner(x, axis, stride):
    return lax.ppermute(x, axis, [(i, i ^ 1 << stride) for i in range(lax.axis_size(axis))])


def item_weights(ratios, pair_list):
    item_index = jnp.arange(ratios.shape[0], dtype=jnp.int32)
    paired = (pair_list[:, None] == pair_list[None, :]) & (
        item_index[:, None] != item_index[None, :]
    )
    partner_ratio = jnp.sum(jnp.where(paired, ratios[None, :], 0.0), axis=1)
    partner_index = jnp.sum(jnp.where(paired, item_index[None, :], 0), axis=1)
    polarity = jnp.where(item_index < partner_index, -1.0, 1.0).astype(ratios.dtype)
    margin = BETA * polarity * (partner_ratio - ratios)
    return polarity * jax.nn.sigmoid(-margin)


def token_weights(weights_item, items_tok):
    choices_row = jnp.arange(weights_item.shape[0], dtype=jnp.int32)
    lookup = jnp.where(items_tok[:, None] == choices_row[None, :], weights_item[None, :], 0.0)
    return jnp.sum(lookup, axis=1)


def attend_mask(rows_item, rows_image, rows_pos, cols_item, cols_image, cols_pos):
    same_item = rows_item[:, None] == cols_item[None, :]
    causal = cols_pos[None, :] <= rows_pos[:, None]
    same_image = (rows_image[:, None] == cols_image[None, :]) & (rows_image[:, None] > 0)
    return same_item & (causal | same_image)


def rows_product(x_part, grads_part):
    return lax.dot_general(
        x_part.astype(jnp.float32),
        grads_part,
        (((0,), (0,)), ((), ())),
        precision=lax.Precision.HIGHEST,
    )


def local(
    input_rows, queries, key_values, out_grad, item_logratio, pair_ids, tile_item, tile_image
):
    x_rows = input_rows[0]
    local_queries = queries[0]
    length = local_queries.shape[0]
    heads_here = local_queries.shape[1] // HD
    group_size = lax.axis_size("tp") // KVH
    tp_index = lax.axis_index("tp")
    kv_index = tp_index // group_size
    kv_cols = lax.dynamic_slice_in_dim(key_values[0], kv_index * 2 * HD, 2 * HD, 1)
    key_rows = kv_cols[:, :HD]
    value_rows = kv_cols[:, HD:]
    items_tok = jnp.repeat(tile_item[0], TILE)
    images_tok = jnp.repeat(tile_image[0], TILE)
    positions = jnp.arange(length, dtype=jnp.int32)
    factors = token_weights(item_weights(item_logratio[0], pair_ids[0]), items_tok)
    weighted = (out_grad[0].astype(jnp.float32) * factors[:, None]).astype(jnp.bfloat16)
    query_heads = local_queries.reshape(length, heads_here, HD)
    weighted_heads = weighted.reshape(length, heads_here, HD)
    span_rows = min(512, length)
    inv_root = 1.0 / math.sqrt(HD)

    def attend_rows(step_index, state_tuple):
        grad_rows, key_grad, value_grad = state_tuple
        first_row = step_index * span_rows
        query_span = lax.dynamic_slice_in_dim(query_heads, first_row, span_rows, 0)
        weighted_span = lax.dynamic_slice_in_dim(weighted_heads, first_row, span_rows, 0)
        allowed = attend_mask(
            lax.dynamic_slice_in_dim(items_tok, first_row, span_rows, 0),
            lax.dynamic_slice_in_dim(images_tok, first_row, span_rows, 0),
            lax.dynamic_slice_in_dim(positions, first_row, span_rows, 0),
            items_tok,
            images_tok,
            positions,
        )[None]
        scores = (
            jnp.einsum("qhd,kd->hqk", query_span, key_rows, preferred_element_type=jnp.float32)
            * inv_root
        )
        scores = jnp.where(allowed, scores, MASKED)
        row_max = jnp.max(scores, axis=2, keepdims=True)
        unnorm = jnp.where(allowed, jnp.exp(scores - row_max), 0.0)
        attend = unnorm / jnp.sum(unnorm, axis=2, keepdims=True)
        attend_low = attend.astype(jnp.bfloat16)
        dprob = jnp.einsum(
            "qhd,kd->hqk", weighted_span, value_rows, preferred_element_type=jnp.float32
        )
        rowdot = jnp.sum(attend * dprob, axis=2, keepdims=True)
        dscore = (attend * (dprob - rowdot)).astype(jnp.bfloat16)
        grad_span = (
            jnp.einsum("hqk,kd->qhd", dscore, key_rows, preferred_element_type=jnp.float32)
            * inv_root
        ).astype(jnp.bfloat16)
        key_grad = (
            key_grad
            + jnp.einsum("hqk,qhd->kd", dscore, query_span, preferred_element_type=jnp.float32)
            * inv_root
        )
        value_grad = value_grad + jnp.einsum(
            "hqk,qhd->kd", attend_low, weighted_span, preferred_element_type=jnp.float32
        )
        grad_rows = lax.dynamic_update_slice_in_dim(grad_rows, grad_span, first_row, 0)
        return (grad_rows, key_grad, value_grad)

    initial = (
        jnp.zeros((length, heads_here, HD), jnp.bfloat16),
        jnp.zeros((length, HD), jnp.float32),
        jnp.zeros((length, HD), jnp.float32),
    )
    grad_rows, key_grad, value_grad = lax.fori_loop(0, length // span_rows, attend_rows, initial)
    grads_kv = jnp.concatenate([key_grad, value_grad], axis=1)
    bit_count = group_size.bit_length() - 1
    whole = rows_product(lax.all_gather(x_rows, "tp", axis=0, tiled=True), grads_kv)
    for bit_level in reversed(range(bit_count)):
        half_cols = whole.shape[1] // 2
        parity = tp_index // 2**bit_level % 2
        kept = lax.dynamic_slice_in_dim(whole, parity * half_cols, half_cols, 1)
        handed = lax.dynamic_slice_in_dim(whole, (1 - parity) * half_cols, half_cols, 1)
        whole = kept + from_partner(handed.astype(jnp.bfloat16), "tp", bit_level).astype(
            handed.dtype
        )
    grad_weight = lax.psum_scatter(whole, "dp", scatter_dimension=0, tiled=True)
    return (grad_rows.reshape(1, length, heads_here * HD), grad_weight)


def solution(mesh):
    in_specs = (
        P("dp", "tp", None),
        P("dp", None, "tp"),
        P("dp", None, None),
        P("dp", None, "tp"),
        P("dp", None),
        P("dp", None),
        P("dp", None),
        P("dp", None),
    )
    out_specs = (P("dp", None, "tp"), P("dp", "tp"))
    return jax.shard_map(local, mesh=mesh, in_specs=in_specs, out_specs=out_specs, check_vma=False)
```

profile of v0, /device:TPU:1, one launch (start us, length us, event | category | flops | bytes accessed | tf_op | source)
XLA Modules:
  0.0 296.8 jit_solution(5522915693293500294)
XLA Ops:
  8.1 2.3 copy.23
  17.5 133.1 %while.19 = (s32[]{:T(128)}, bf16[2048,2,128]{2,1,0:T(2,128)(2,1)}, f32[2048,128]{1,0:T(8,128)S(1)}, f32[2048,128]{1,0:T(8,128)}, s32[2048]{0:T(1024)S(1)}, /*in...) while((s32[]{:T(128)}, bf16[2048,2,128]{2,1,0:T(2,128)(2,1)}, ...), condition=%wide.region_7.8_spmd.clone.clone, body=%wide.region_3.7_spmd.clone.clone.sunk | while | flops 2721580544 | bytes 126176792 | solution.py:125
  17.8 2.0 or_and_fusion.2
  19.8 8.7 %fusion.102 = (f32[2,512]{1,0:T(2,128)S(1)}, f32[2,512,2048]{2,1,0:T(8,128)}) fusion(pred[512,2048]{1,0:T(8,128)(4,1)S(1)} %or_and_fusion.2, bf16[2048,128]{1,0:T(8,128)(2,1)} %get-tuple-element.503, bf16[2048,2,128]{0,2,1:T(8,128)(2,1)S(1)} %get-tuple-element.502, s32[]{:T(128)S(6)} %select_n.135), kind=kOutput, calls=%fused_computation.80.clone.1 | convolution fusion | flops 547358720 | bytes 11276292 | tf_op jit(solution)/shard_map/while/body/eval_jaxpr/sub | solution.py:97
  28.4 5.9 %fusion.103 = (f32[2,512]{1,0:T(2,128)S(1)}, f32[512,2,2048]{2,0,1:T(8,128)S(1)}) fusion(f32[2,512,2048]{2,1,0:T(8,128)} %get-tuple-element.457, f32[2,512]{1,0:T(2,128)S(1)} %get-tuple-element.458, bf16[2048,128]{1,0:T(8,128)(2,1)} %get-tuple-element.505, bf16[2048,2,128]{0,2,1:T(8,128)(2,1)} %get-tuple-element.504, s32[]{:T(128)S(6)} %select_n.135), kind=kOutput, calls=%fused_computation.5.clone.1 | convolution fusion | flops 543161344 | bytes 17571844 | tf_op jit(solution)/shard_map/while/body/eval_jaxpr/qhd,kd->hqk/dot_general | solution.py:100
  36.2 2.0 copy-done
  40.4 4.1 %fusion.106 = f32[2048,128]{1,0:T(8,128)S(1)} fusion(bf16[2,512,2048]{2,1,0:T(8,128)(2,1)} %copy-done, f32[2048,128]{1,0:T(8,128)S(1)} %get-tuple-element.480, pred[]{:T(512)S(6)} %compare.10, bf16[2048,2,128]{0,2,1:T(8,128)(2,1)S(1)} %get-tuple-element.502, s32[]{:T(128)S(6)} %select_n.135), kind=kOutput, calls=%fused_computation.24.clone.1 | convolution fusion | flops 537657344 | bytes 6553605 | tf_op jit(solution)/shard_map/while/body/eval_jaxpr/hqk,qhd->kd/dot_general | solution.py:111
  44.5 5.5 %fusion.107 = f32[2048,128]{1,0:T(8,128)S(1)} fusion(f32[2048,128]{1,0:T(8,128)S(1)} %copy-done.9, pred[]{:T(512)S(6)} %compare.10, bf16[2048,2,128]{0,2,1:T(8,128)(2,1)} %get-tuple-element.504, s32[]{:T(128)S(6)} %select_n.135, f32[2,512,2048]{2,1,0:T(8,128)} %get-tuple-element.457, f32[2,512]{1,0:T(2,128)S(1)} %get-tuple-element.458), kind=kOutput, calls=%fused_computation.25.clone.1 | convolution fusion | flops 541589504 | bytes 10752005 | tf_op jit(solution)/shard_map/while/body/eval_jaxpr/hqk,qhd->kd/dot_general | solution.py:114
  51.3 2.0 or_and_fusion.2
  53.3 8.6 %fusion.102 = (f32[2,512]{1,0:T(2,128)S(1)}, f32[2,512,2048]{2,1,0:T(8,128)}) fusion(pred[512,2048]{1,0:T(8,128)(4,1)S(1)} %or_and_fusion.2, bf16[2048,128]{1,0:T(8,128)(2,1)} %get-tuple-element.503, bf16[2048,2,128]{0,2,1:T(8,128)(2,1)S(1)} %get-tuple-element.502, s32[]{:T(128)S(6)} %select_n.135), kind=kOutput, calls=%fused_computation.80.clone.1 | convolution fusion | flops 547358720 | bytes 11276292 | tf_op jit(solution)/shard_map/while/body/eval_jaxpr/sub | solution.py:97
  61.9 5.9 %fusion.103 = (f32[2,512]{1,0:T(2,128)S(1)}, f32[512,2,2048]{2,0,1:T(8,128)S(1)}) fusion(f32[2,512,2048]{2,1,0:T(8,128)} %get-tuple-element.457, f32[2,512]{1,0:T(2,128)S(1)} %get-tuple-element.458, bf16[2048,128]{1,0:T(8,128)(2,1)} %get-tuple-element.505, bf16[2048,2,128]{0,2,1:T(8,128)(2,1)} %get-tuple-element.504, s32[]{:T(128)S(6)} %select_n.135), kind=kOutput, calls=%fused_computation.5.clone.1 | convolution fusion | flops 543161344 | bytes 17571844 | tf_op jit(solution)/shard_map/while/body/eval_jaxpr/qhd,kd->hqk/dot_general | solution.py:100
  69.6 2.0 copy-done
  73.8 4.1 %fusion.106 = f32[2048,128]{1,0:T(8,128)S(1)} fusion(bf16[2,512,2048]{2,1,0:T(8,128)(2,1)} %copy-done, f32[2048,128]{1,0:T(8,128)S(1)} %get-tuple-element.480, pred[]{:T(512)S(6)} %compare.10, bf16[2048,2,128]{0,2,1:T(8,128)(2,1)S(1)} %get-tuple-element.502, s32[]{:T(128)S(6)} %select_n.135), kind=kOutput, calls=%fused_computation.24.clone.1 | convolution fusion | flops 537657344 | bytes 6553605 | tf_op jit(solution)/shard_map/while/body/eval_jaxpr/hqk,qhd->kd/dot_general | solution.py:111
  77.9 5.5 %fusion.107 = f32[2048,128]{1,0:T(8,128)S(1)} fusion(f32[2048,128]{1,0:T(8,128)S(1)} %copy-done.9, pred[]{:T(512)S(6)} %compare.10, bf16[2048,2,128]{0,2,1:T(8,128)(2,1)} %get-tuple-element.504, s32[]{:T(128)S(6)} %select_n.135, f32[2,512,2048]{2,1,0:T(8,128)} %get-tuple-element.457, f32[2,512]{1,0:T(2,128)S(1)} %get-tuple-element.458), kind=kOutput, calls=%fused_computation.25.clone.1 | convolution fusion | flops 541589504 | bytes 10752005 | tf_op jit(solution)/shard_map/while/body/eval_jaxpr/hqk,qhd->kd/dot_general | solution.py:114
  84.7 2.0 or_and_fusion.2
  86.7 8.6 %fusion.102 = (f32[2,512]{1,0:T(2,128)S(1)}, f32[2,512,2048]{2,1,0:T(8,128)}) fusion(pred[512,2048]{1,0:T(8,128)(4,1)S(1)} %or_and_fusion.2, bf16[2048,128]{1,0:T(8,128)(2,1)} %get-tuple-element.503, bf16[2048,2,128]{0,2,1:T(8,128)(2,1)S(1)} %get-tuple-element.502, s32[]{:T(128)S(6)} %select_n.135), kind=kOutput, calls=%fused_computation.80.clone.1 | convolution fusion | flops 547358720 | bytes 11276292 | tf_op jit(solution)/shard_map/while/body/eval_jaxpr/sub | solution.py:97
  95.3 5.9 %fusion.103 = (f32[2,512]{1,0:T(2,128)S(1)}, f32[512,2,2048]{2,0,1:T(8,128)S(1)}) fusion(f32[2,512,2048]{2,1,0:T(8,128)} %get-tuple-element.457, f32[2,512]{1,0:T(2,128)S(1)} %get-tuple-element.458, bf16[2048,128]{1,0:T(8,128)(2,1)} %get-tuple-element.505, bf16[2048,2,128]{0,2,1:T(8,128)(2,1)} %get-tuple-element.504, s32[]{:T(128)S(6)} %select_n.135), kind=kOutput, calls=%fused_computation.5.clone.1 | convolution fusion | flops 543161344 | bytes 17571844 | tf_op jit(solution)/shard_map/while/body/eval_jaxpr/qhd,kd->hqk/dot_general | solution.py:100
  103.0 2.0 copy-done
  107.2 4.1 %fusion.106 = f32[2048,128]{1,0:T(8,128)S(1)} fusion(bf16[2,512,2048]{2,1,0:T(8,128)(2,1)} %copy-done, f32[2048,128]{1,0:T(8,128)S(1)} %get-tuple-element.480, pred[]{:T(512)S(6)} %compare.10, bf16[2048,2,128]{0,2,1:T(8,128)(2,1)S(1)} %get-tuple-element.502, s32[]{:T(128)S(6)} %select_n.135), kind=kOutput, calls=%fused_computation.24.clone.1 | convolution fusion | flops 537657344 | bytes 6553605 | tf_op jit(solution)/shard_map/while/body/eval_jaxpr/hqk,qhd->kd/dot_general | solution.py:111
  111.3 5.3 %fusion.107 = f32[2048,128]{1,0:T(8,128)S(1)} fusion(f32[2048,128]{1,0:T(8,128)S(1)} %copy-done.9, pred[]{:T(512)S(6)} %compare.10, bf16[2048,2,128]{0,2,1:T(8,128)(2,1)} %get-tuple-element.504, s32[]{:T(128)S(6)} %select_n.135, f32[2,512,2048]{2,1,0:T(8,128)} %get-tuple-element.457, f32[2,512]{1,0:T(2,128)S(1)} %get-tuple-element.458), kind=kOutput, calls=%fused_computation.25.clone.1 | convolution fusion | flops 541589504 | bytes 10752005 | tf_op jit(solution)/shard_map/while/body/eval_jaxpr/hqk,qhd->kd/dot_general | solution.py:114
  117.9 2.0 or_and_fusion.2
  119.9 8.6 %fusion.102 = (f32[2,512]{1,0:T(2,128)S(1)}, f32[2,512,2048]{2,1,0:T(8,128)}) fusion(pred[512,2048]{1,0:T(8,128)(4,1)S(1)} %or_and_fusion.2, bf16[2048,128]{1,0:T(8,128)(2,1)} %get-tuple-element.503, bf16[2048,2,128]{0,2,1:T(8,128)(2,1)S(1)} %get-tuple-element.502, s32[]{:T(128)S(6)} %select_n.135), kind=kOutput, calls=%fused_computation.80.clone.1 | convolution fusion | flops 547358720 | bytes 11276292 | tf_op jit(solution)/shard_map/while/body/eval_jaxpr/sub | solution.py:97
  128.5 5.8 %fusion.103 = (f32[2,512]{1,0:T(2,128)S(1)}, f32[512,2,2048]{2,0,1:T(8,128)S(1)}) fusion(f32[2,512,2048]{2,1,0:T(8,128)} %get-tuple-element.457, f32[2,512]{1,0:T(2,128)S(1)} %get-tuple-element.458, bf16[2048,128]{1,0:T(8,128)(2,1)} %get-tuple-element.505, bf16[2048,2,128]{0,2,1:T(8,128)(2,1)} %get-tuple-element.504, s32[]{:T(128)S(6)} %select_n.135), kind=kOutput, calls=%fused_computation.5.clone.1 | convolution fusion | flops 543161344 | bytes 17571844 | tf_op jit(solution)/shard_map/while/body/eval_jaxpr/qhd,kd->hqk/dot_general | solution.py:100
  140.2 4.1 %fusion.106 = f32[2048,128]{1,0:T(8,128)S(1)} fusion(bf16[2,512,2048]{2,1,0:T(8,128)(2,1)} %copy-done, f32[2048,128]{1,0:T(8,128)S(1)} %get-tuple-element.480, pred[]{:T(512)S(6)} %compare.10, bf16[2048,2,128]{0,2,1:T(8,128)(2,1)S(1)} %get-tuple-element.502, s32[]{:T(128)S(6)} %select_n.135), kind=kOutput, calls=%fused_computation.24.clone.1 | convolution fusion | flops 537657344 | bytes 6553605 | tf_op jit(solution)/shard_map/while/body/eval_jaxpr/hqk,qhd->kd/dot_general | solution.py:111
  144.2 5.3 %fusion.107 = f32[2048,128]{1,0:T(8,128)S(1)} fusion(f32[2048,128]{1,0:T(8,128)S(1)} %copy-done.9, pred[]{:T(512)S(6)} %compare.10, bf16[2048,2,128]{0,2,1:T(8,128)(2,1)} %get-tuple-element.504, s32[]{:T(128)S(6)} %select_n.135, f32[2,512,2048]{2,1,0:T(8,128)} %get-tuple-element.457, f32[2,512]{1,0:T(2,128)S(1)} %get-tuple-element.458), kind=kOutput, calls=%fused_computation.25.clone.1 | convolution fusion | flops 541589504 | bytes 10752005 | tf_op jit(solution)/shard_map/while/body/eval_jaxpr/hqk,qhd->kd/dot_general | solution.py:114
  150.6 16.4 %fusion.56 = f32[256,4096]{1,0:T(8,128)S(1)} fusion(bf16[1,2048,4096]{2,1,0:T(8,128)(2,1)} %all-gather.3.cloned.1.call-done, f32[2048,128]{1,0:T(8,128)} %get-tuple-element.223, f32[2048,128]{1,0:T(8,128)S(1)} %get-tuple-element.222), kind=kOutput, calls=%fused_computation.52 | convolution fusion | flops 25770328064 | bytes 23068672 | tf_op jit(solution)/shard_map/dot_general | solution.py:47
  169.1 2.8 collective-permute-start
  171.9 21.8 %collective-permute-done = bf16[4096,128]{0,1:T(8,128)(2,1)} collective-permute-done((bf16[4096,128]{0,1:T(8,128)(2,1)S(1)}, bf16[4096,128]{0,1:T(8,128)(2,1)}, u32[]{:S(2)}, u32[]{:S(2)}) %collective-permute-start) | collective-permute-done | bytes 1048608 | tf_op jit(solution)/shard_map/ppermute | solution.py:18
  193.7 2.1 bitcast_add_fusion
  196.7 2.4 collective-permute-start.1
  201.0 2.1 convert_add_fusion
  204.6 85.4 %reduce-scatter.2.cloned.1.call-done = f32[256,64]{0,1:T(8,128)} async-done(((f32[4096,64]{0,1:T(8,128)}), f32[256,64]{0,1:T(8,128)}) %reduce-scatter.2.cloned.1.call-update) | async-done | bytes 65552 | tf_op jit(solution)/shard_map/reduce_scatter | solution.py:137
  (113 shorter events, 37.1 us)
Async XLA Ops:
  7.2 4.7 %copy-start.7 = (s32[1,4]{1,0:T(1,128)S(1)}, s32[1,4]{1,0:T(1,128)}, u32[]{:S(2)}) copy-start(s32[1,4]{1,0:T(1,128)} %param.15) | copy-start | bytes 52
  7.2 4.9 %copy-start.8 = (f32[1,4]{1,0:T(1,128)S(1)}, f32[1,4]{1,0:T(1,128)}, u32[]{:S(2)}) copy-start(f32[1,4]{1,0:T(1,128)} %param.14) | copy-start | bytes 52
  7.2 5.1 %copy-start.6 = (s32[1,16]{1,0:T(1,128)S(1)}, s32[1,16]{1,0:T(1,128)}, u32[]{:S(2)}) copy-start(s32[1,16]{1,0:T(1,128)} %param.16) | copy-start | bytes 196
  7.2 5.1 %copy-start.5 = (s32[1,16]{1,0:T(1,128)S(1)}, s32[1,16]{1,0:T(1,128)}, u32[]{:S(2)}) copy-start(s32[1,16]{1,0:T(1,128)} %param.17) | copy-start | bytes 196
  7.2 143.4 %all-gather.3.cloned.1.call-start = ((), (), s32[]{:S(2)}) async-start(), calls=%async_computation.2 | async-start | bytes 17825792 | tf_op jit(solution)/shard_map/all_gather | solution.py:128
  7.9 282.0 %reduce-scatter.2.cloned.1.call-start = ((), (), s32[]{:S(2)}) async-start(), calls=%async_computation.1 | async-start | bytes 1114112 | tf_op jit(solution)/shard_map/reduce_scatter | solution.py:137
  11.8 3.0 copy-start.1
  28.4 5.9 %slice-start = ((s8[8388608]{0:T(1024)(128)(4,1)}), s8[4194304]{0:T(1024)(128)(4,1)S(1)}, s32[]{:S(2)}) async-start(s8[8388608]{0:T(1024)(128)(4,1)} %bitcast.122), calls=%async_computation.3 | async-start | bytes 8388608 | tf_op jit(solution)/shard_map/while
  28.4 6.4 %slice-start.1 = ((s8[8388608]{0:T(1024)(128)(4,1)}), s8[4194304]{0:T(1024)(128)(4,1)S(1)}, s32[]{:S(2)}) async-start(s8[8388608]{0:T(1024)(128)(4,1)} %bitcast.122), calls=%async_computation.4 | async-start | bytes 8388608 | tf_op jit(solution)/shard_map/while
  34.8 3.4 %copy-start.4 = (bf16[2048,128]{1,0:T(8,128)(2,1)S(1)}, bf16[2048,128]{1,0:T(8,128)(2,1)}, u32[]{:S(2)}) copy-start(bf16[2048,128]{1,0:T(8,128)(2,1)} %get-tuple-element.503) | copy-start | bytes 1572868 | tf_op jit(solution)/shard_map/while
  36.2 2.0 copy-start
  40.4 4.1 %copy-start.9 = (f32[2048,128]{1,0:T(8,128)S(1)}, f32[2048,128]{1,0:T(8,128)}, u32[]{:S(2)}) copy-start(f32[2048,128]{1,0:T(8,128)} %get-tuple-element.481) | copy-start | bytes 3145732 | tf_op jit(solution)/shard_map/while
  61.9 6.0 %slice-start = ((s8[8388608]{0:T(1024)(128)(4,1)}), s8[4194304]{0:T(1024)(128)(4,1)S(1)}, s32[]{:S(2)}) async-start(s8[8388608]{0:T(1024)(128)(4,1)} %bitcast.122), calls=%async_computation.3 | async-start | bytes 8388608 | tf_op jit(solution)/shard_map/while
  61.9 6.3 %slice-start.1 = ((s8[8388608]{0:T(1024)(128)(4,1)}), s8[4194304]{0:T(1024)(128)(4,1)S(1)}, s32[]{:S(2)}) async-start(s8[8388608]{0:T(1024)(128)(4,1)} %bitcast.122), calls=%async_computation.4 | async-start | bytes 8388608 | tf_op jit(solution)/shard_map/while
  68.2 3.4 %copy-start.4 = (bf16[2048,128]{1,0:T(8,128)(2,1)S(1)}, bf16[2048,128]{1,0:T(8,128)(2,1)}, u32[]{:S(2)}) copy-start(bf16[2048,128]{1,0:T(8,128)(2,1)} %get-tuple-element.503) | copy-start | bytes 1572868 | tf_op jit(solution)/shard_map/while
  69.6 2.0 copy-start
  73.8 4.1 %copy-start.9 = (f32[2048,128]{1,0:T(8,128)S(1)}, f32[2048,128]{1,0:T(8,128)}, u32[]{:S(2)}) copy-start(f32[2048,128]{1,0:T(8,128)} %get-tuple-element.481) | copy-start | bytes 3145732 | tf_op jit(solution)/shard_map/while
  95.3 5.9 %slice-start = ((s8[8388608]{0:T(1024)(128)(4,1)}), s8[4194304]{0:T(1024)(128)(4,1)S(1)}, s32[]{:S(2)}) async-start(s8[8388608]{0:T(1024)(128)(4,1)} %bitcast.122), calls=%async_computation.3 | async-start | bytes 8388608 | tf_op jit(solution)/shard_map/while
  95.3 6.3 %slice-start.1 = ((s8[8388608]{0:T(1024)(128)(4,1)}), s8[4194304]{0:T(1024)(128)(4,1)S(1)}, s32[]{:S(2)}) async-start(s8[8388608]{0:T(1024)(128)(4,1)} %bitcast.122), calls=%async_computation.4 | async-start | bytes 8388608 | tf_op jit(solution)/shard_map/while
  101.6 3.4 %copy-start.4 = (bf16[2048,128]{1,0:T(8,128)(2,1)S(1)}, bf16[2048,128]{1,0:T(8,128)(2,1)}, u32[]{:S(2)}) copy-start(bf16[2048,128]{1,0:T(8,128)(2,1)} %get-tuple-element.503) | copy-start | bytes 1572868 | tf_op jit(solution)/shard_map/while
  103.0 2.0 copy-start
  107.2 4.1 %copy-start.9 = (f32[2048,128]{1,0:T(8,128)S(1)}, f32[2048,128]{1,0:T(8,128)}, u32[]{:S(2)}) copy-start(f32[2048,128]{1,0:T(8,128)} %get-tuple-element.481) | copy-start | bytes 3145732 | tf_op jit(solution)/shard_map/while
  116.6 1.0 copy-start.10
  128.5 5.8 %slice-start = ((s8[8388608]{0:T(1024)(128)(4,1)}), s8[4194304]{0:T(1024)(128)(4,1)S(1)}, s32[]{:S(2)}) async-start(s8[8388608]{0:T(1024)(128)(4,1)} %bitcast.122), calls=%async_computation.3 | async-start | bytes 8388608 | tf_op jit(solution)/shard_map/while
  128.5 6.1 %slice-start.1 = ((s8[8388608]{0:T(1024)(128)(4,1)}), s8[4194304]{0:T(1024)(128)(4,1)S(1)}, s32[]{:S(2)}) async-start(s8[8388608]{0:T(1024)(128)(4,1)} %bitcast.122), calls=%async_computation.4 | async-start | bytes 8388608 | tf_op jit(solution)/shard_map/while
  134.6 3.4 %copy-start.4 = (bf16[2048,128]{1,0:T(8,128)(2,1)S(1)}, bf16[2048,128]{1,0:T(8,128)(2,1)}, u32[]{:S(2)}) copy-start(bf16[2048,128]{1,0:T(8,128)(2,1)} %get-tuple-element.503) | copy-start | bytes 1572868 | tf_op jit(solution)/shard_map/while
  135.9 2.0 copy-start
  140.2 4.1 %copy-start.9 = (f32[2048,128]{1,0:T(8,128)S(1)}, f32[2048,128]{1,0:T(8,128)}, u32[]{:S(2)}) copy-start(f32[2048,128]{1,0:T(8,128)} %get-tuple-element.481) | copy-start | bytes 3145732 | tf_op jit(solution)/shard_map/while
  167.0 1.9 copy-start.3
  169.1 24.6 %collective-permute-start = (bf16[4096,128]{0,1:T(8,128)(2,1)S(1)}, bf16[4096,128]{0,1:T(8,128)(2,1)}, u32[]{:S(2)}, u32[]{:S(2)}) collective-permute-start(bf16[4096,128]{0,1:T(8,128)(2,1)S(1)} %fusion.62), channel_id=1, source_target_pairs={{0,2},{1,3},{2,0},{3,1},{4,6},{5,7},{6,4},{7,5},{8,10},{9,11},{10,... | collective-permute-start | bytes 3145736 | tf_op jit(solution)/shard_map/ppermute | solution.py:18
  171.9 31.2 %copy-start.2 = (bf16[2048,2,128]{2,1,0:T(2,128)(2,1)S(1)}, bf16[2048,2,128]{2,1,0:T(2,128)(2,1)}, u32[]{:S(2)}) copy-start(bf16[2048,2,128]{2,1,0:T(2,128)(2,1)} %get-tuple-element.221) | copy-start | bytes 3145732
  196.7 4.3 %collective-permute-start.1 = (bf16[4096,64]{0,1:T(8,128)(2,1)}, bf16[4096,64]{0,1:T(8,128)(2,1)}, u32[]{:S(2)}, u32[]{:S(2)}) collective-permute-start(bf16[4096,64]{0,1:T(8,128)(2,1)} %dynamic-slice_convert_fusion.1), channel_id=1, source_target_pairs={{0,1},{1,0},{2,3},{3,2},{4,5},{5,4},{6,7},{7,6},{8,9},{9,8},{10,11... | collective-permute-start | bytes 1572872 | tf_op jit(solution)/shard_map/ppermute | solution.py:18
  (3 other events, 2.9 us)
Sparse Core Ops, SparseCore 0:
  9.9 98.4 all-gather.2
  203.2 86.7 reduce-scatter.1
where the time goes:
time: 298 us; the launch traced here: 297 us
  matrix products  117 us (39%)
  waiting for transfers between devices  110 us (37%)
  local copies, waits for them, and re-layouts  30.1 us (10%)
  other arithmetic  19.8 us (7%)
  between operations  14.2 us (5%)
  starting transfers between devices  5.25 us (2%)
    reduce_scatter x1, waiting for transfers between devices, local(): grad_weight = lax.psum_scatter(whole, 'dp', scatter_dimension=0, tiled=True)  85.4 us
    sub x4, matrix products, attend_rows(): unnorm = jnp.where(allowed, jnp.exp(scores - row_max), 0.0)  34.4 us
    ppermute x2, waiting for transfers between devices, from_partner(): lax.ppermute(x, axis, [(i, i ^ 1 << stride) for i in range(lax.axis_size(...  23.7 us
    dot_general x4, matrix products, attend_rows(): jnp.einsum('qhd,kd->hqk', weighted_span, value_rows, preferred_element_ty...  23.6 us
    dot_general x4, matrix products, attend_rows(): jnp.einsum('hqk,qhd->kd', attend_low, weighted_span, preferred_element_ty...  21.6 us
    dot_general x1, matrix products, rows_product(): lax.dot_general(x_part.astype(jnp.float32), grads_part, (((0,), (0,)), ((...  16.4 us
    dot_general x4, matrix products, attend_rows(): jnp.einsum('hqk,qhd->kd', dscore, query_span, preferred_element_type=jnp....  16.3 us
    while x48, local copies, waits for them, and re-layouts  13.3 us
  transfers between devices with their start and end apart: 4, of which 3 were waited for; matrix products, arithmetic and copies ran while one was open for 44% of the time, Pallas kernels for 0%

commit v1 on v0

v1 whole, which is shorter than its diff:
```python
import functools, math
import jax, jax.numpy as jnp
from jax import lax
from jax.experimental import pallas as pl
from jax.experimental.pallas import tpu as pltpu

from jax.sharding import PartitionSpec as P

KVH = 4; HD = 128; TILE = 128; BETA = 0.1
MASKED = -1e30
LOG2E = 1.4426950408889634

def attention_kernel(ratio, pair, item, image, q_ref, og_ref, kv_hbm, dq_ref, kvt_ref,
                     kv, s_scr, dp_scr, acc, lo_s, hi_s, z_s, kv_sem):
    group = lax.axis_size("tp") // KVH
    g = lax.axis_index("tp") // group
    load = pltpu.make_async_copy(kv_hbm.at[0, :, pl.ds(pl.multiple_of(g * 2 * HD, 2 * HD), 2 * HD)], kv, kv_sem)
    load.start()
    nt = 16
    items = ratio.shape[1]
    inv_root = 1.0 / math.sqrt(HD)
    c2 = inv_root * LOG2E
    acc[...] = jnp.zeros_like(acc)
    lo_s[0] = 0
    for i in range(1, nt):
        lo_s[i] = jnp.where(item[0, i] == item[0, i - 1], lo_s[i - 1], i)
    hi_s[nt - 1] = nt - 1
    for i in reversed(range(nt - 1)):
        same = (image[0, i] > 0) & (image[0, i] == image[0, i + 1]) & (item[0, i] == item[0, i + 1])
        hi_s[i] = jnp.where(same, hi_s[i + 1], i)
    for a in range(items):
        other = jnp.float32(0.0)
        p = jnp.float32(1.0)
        for b in range(items):
            if b != a:
                same = pair[0, a] == pair[0, b]
                other = other + jnp.where(same, ratio[0, b], 0.0)
                if a < b:
                    p = jnp.where(same, -1.0, p)
        z_s[a] = BETA * p * (other - ratio[0, a])
        z_s[items + a] = p
    load.wait()

    def row_tile(I, carry):
        lo = lo_s[I]
        hi = hi_s[I]
        img = image[0, I]
        it = item[0, I]
        r0 = pl.multiple_of(I * TILE, TILE)
        qi = q_ref[0, pl.ds(r0, TILE), :]
        q2 = jnp.concatenate([qi[:, :HD], qi[:, HD:]], axis=0)
        coef = z_s[items + it] / (1.0 + jnp.exp(jnp.full((8, HD), z_s[it], jnp.float32)))
        coef = jnp.concatenate([coef[:1], coef[:1]], axis=1)
        wi = (og_ref[0, pl.ds(r0, TILE), :].astype(jnp.float32) * coef).astype(jnp.bfloat16)
        w2 = jnp.concatenate([wi[:, :HD], wi[:, HD:]], axis=0)
        q2t = q2.T
        w2t = w2.T
        tiles = hi - lo + 1
        chunks = (tiles + 1) // 2

        def body(n):
            st_t = jnp.minimum(lo, nt - 2 * n)
            st = pl.multiple_of(st_t * TILE, TILE)
            W = 2 * TILE
            row = lax.broadcasted_iota(jnp.int32, (TILE, 1), 0)
            row = jnp.concatenate([row, row], axis=0)
            first = lo * TILE - st
            last = jnp.where(img > 0, jnp.full((2 * TILE, 1), (hi + 1) * TILE - 1 - st), r0 - st + row)
            m = None
            for ch in range(n):
                kc = kv[pl.ds(st + ch * W, W), :HD]
                vc = kv[pl.ds(st + ch * W, W), HD:]
                s = lax.dot_general(q2, kc, (((1,), (1,)), ((), ())), preferred_element_type=jnp.float32)
                if ch == 0 or ch == n - 1:
                    col = lax.broadcasted_iota(jnp.int32, (1, W), 1) + ch * W
                    ok = col <= last
                    if ch == 0 or n == 1:
                        ok = ok & (col >= first)
                    s = jnp.where(ok, s, MASKED)
                s_scr[:, ch * W:(ch + 1) * W] = s
                mm = jnp.maximum(s[:, :HD], s[:, HD:])
                m = mm if m is None else jnp.maximum(m, mm)
                dp_scr[:, ch * W:(ch + 1) * W] = lax.dot_general(w2, vc, (((1,), (1,)), ((), ())), preferred_element_type=jnp.float32)
            mr = jnp.max(m, axis=1, keepdims=True) * c2
            l = None
            for ch in range(n):
                p = jnp.exp2(s_scr[:, ch * W:(ch + 1) * W] * c2 - mr)
                s_scr[:, ch * W:(ch + 1) * W] = p
                pd = p * dp_scr[:, ch * W:(ch + 1) * W]
                ll = p[:, :HD] + p[:, HD:]
                rr = pd[:, :HD] + pd[:, HD:]
                l = ll if l is None else l + ll
                r = rr if ch == 0 else r + rr
            inv = 1.0 / jnp.sum(l, axis=1, keepdims=True)
            rd = jnp.sum(r, axis=1, keepdims=True) * inv
            dq = None
            for ch in range(n):
                kc = kv[pl.ds(st + ch * W, W), :HD]
                at = s_scr[:, ch * W:(ch + 1) * W] * inv
                ds = (at * (dp_scr[:, ch * W:(ch + 1) * W] - rd)).astype(jnp.bfloat16)
                at = at.astype(jnp.bfloat16)
                d = jnp.dot(ds, kc, preferred_element_type=jnp.float32)
                dq = d if dq is None else dq + d
                cols = pl.ds(st + ch * W, W)
                acc[:HD, cols] += jnp.dot(q2t, ds, preferred_element_type=jnp.float32)
                acc[HD:, cols] += jnp.dot(w2t, at, preferred_element_type=jnp.float32)
            dq = (dq * inv_root).astype(jnp.bfloat16)
            dq_ref[0, pl.ds(r0, TILE), :HD] = dq[:TILE]
            dq_ref[0, pl.ds(r0, TILE), HD:] = dq[TILE:]

        for n in range(1, nt // 2 + 1):
            @pl.when(chunks == n)
            def _():
                body(n)
        return carry

    lax.fori_loop(0, nt, row_tile, 0)
    kvt_ref[:HD] = (acc[:HD] * inv_root).astype(jnp.bfloat16)
    kvt_ref[HD:] = acc[HD:].astype(jnp.bfloat16)


def attention(queries, out_grad, key_values, ratio, pair, item, image):
    L = queries.shape[1]
    nt = L // TILE
    smem = pl.BlockSpec(memory_space=pltpu.SMEM)
    vmem = pl.BlockSpec(memory_space=pltpu.VMEM)
    return pl.pallas_call(
        attention_kernel,
        out_shape=[jax.ShapeDtypeStruct(queries.shape, jnp.bfloat16),
                   jax.ShapeDtypeStruct((2 * HD, L), jnp.bfloat16)],
        in_specs=[smem] * 4 + [vmem, vmem, pl.BlockSpec(memory_space=pl.ANY)],
        out_specs=[vmem, vmem],
        scratch_shapes=[
            pltpu.VMEM((L, 2 * HD), jnp.bfloat16),
            pltpu.VMEM((2 * TILE, L), jnp.float32),
            pltpu.VMEM((2 * TILE, L), jnp.float32),
            pltpu.VMEM((2 * HD, L), jnp.float32),
            pltpu.SMEM((nt,), jnp.int32),
            pltpu.SMEM((nt,), jnp.int32),
            pltpu.SMEM((2 * ratio.shape[1],), jnp.float32),
            pltpu.SemaphoreType.DMA,
        ],
        compiler_params=pltpu.CompilerParams(vmem_limit_bytes=48 << 20),
        cost_estimate=pl.CostEstimate(flops=10 * 10**9, bytes_accessed=8 << 20, transcendentals=0),
        name="attention",
    )(ratio, pair, item, image, queries, out_grad, key_values)


def local(input_rows, queries, key_values, out_grad, item_logratio, pair_ids, tile_item, tile_image):
    tp = lax.axis_size("tp")
    t = lax.axis_index("tp")
    xc = lax.all_to_all(input_rows[0], "tp", 1, 0, tiled=True)
    dq, part = attention(queries, out_grad, key_values, item_logratio, pair_ids, tile_item, tile_image)
    for bit in (1, 0):
        half = part.shape[0] // 2
        mine = t // 2**bit % 2
        kept = lax.dynamic_slice_in_dim(part, mine * half, half, 0)
        sent = lax.dynamic_slice_in_dim(part, (1 - mine) * half, half, 0)
        got = lax.ppermute(sent, "tp", [(i, i ^ 1 << bit) for i in range(tp)])
        part = (kept.astype(jnp.float32) + got.astype(jnp.float32)).astype(jnp.bfloat16)
    whole = lax.all_gather(part, "tp", axis=0, tiled=True)
    wt = jnp.dot(whole, xc, preferred_element_type=jnp.float32)
    wt = lax.psum_scatter(wt, "dp", scatter_dimension=0, tiled=True)
    wt = lax.ppermute(wt, ("dp", "tp"), [(a * tp + b, b * tp + a) for a in range(tp) for b in range(tp)])
    return dq, wt.T


def solution(mesh):
    in_specs = (P("dp", "tp", None), P("dp", None, "tp"), P("dp", None, None), P("dp", None, "tp"),
                P("dp", None), P("dp", None), P("dp", None), P("dp", None))
    out_specs = (P("dp", None, "tp"), P("dp", "tp"))
    return jax.shard_map(local, mesh=mesh, in_specs=in_specs, out_specs=out_specs, check_vma=False)
```

time: 298 us -> 209 us (0.70)
  the two profiles are of different devices: /device:TPU:1 before, /device:TPU:36 now
where the time goes in v1:
time: 209 us
  waiting for transfers between devices  137 us (66%)
  Pallas kernels  19.4 us (9%)
  blocking collectives  19.3 us (9%)
  between operations  14.2 us (7%)
  local copies, waits for them, and re-layouts  6.96 us (3%)
  starting transfers between devices  6.59 us (3%)
  matrix products  4.42 us (2%)
    reduce_scatter x1, waiting for transfers between devices, local(): wt = lax.psum_scatter(wt, 'dp', scatter_dimension=0, tiled=True)  89.7 us
    all_gather x1, waiting for transfers between devices, local(): whole = lax.all_gather(part, 'tp', axis=0, tiled=True)  24.6 us
    pallas_call x1, Pallas kernels, attention(): pl.pallas_call(attention_kernel, out_shape=[jax.ShapeDtypeStruct(queries....  19.4 us
    all_to_all x1, blocking collectives, local(): xc = lax.all_to_all(input_rows[0], 'tp', 1, 0, tiled=True)  19.3 us
    ppermute x2, waiting for transfers between devices, local(): got = lax.ppermute(sent, 'tp', [(i, i ^ 1 << bit) for i in range(tp)])  15.1 us
    ppermute x1, waiting for transfers between devices, local(): lax.ppermute(wt, ('dp', 'tp'), [(a * tp + b, b * tp + a) for a in range(t...  7.95 us
    unnamed x16, local copies, waits for them, and re-layouts  6.36 us
    ppermute x1, starting transfers between devices, local(): lax.ppermute(wt, ('dp', 'tp'), [(a * tp + b, b * tp + a) for a in range(t...  6.22 us
  transfers between devices with their start and end apart: 5, of which 5 were waited for; matrix products, arithmetic and copies ran while one was open for 1% of the time, Pallas kernels for 0%

profile of v1, /device:TPU:36, one launch (start us, length us, event | category | flops | bytes accessed | tf_op | source)
XLA Modules:
  0.0 209.1 jit_solution(4964119770846794497)
XLA Ops:
  7.2 0.0 all-gather.2.cloned.1.call-start
  7.2 0.0 copy-start
  7.3 1.2 copy-done
  8.5 0.0 copy-start.1
  8.5 1.2 copy-done.1
  9.7 0.0 copy-start.2
  9.7 0.7 copy-done.2
  10.4 0.0 copy-start.3
  10.4 0.7 copy-done.3
  11.0 0.7 copy-done.4
  11.7 0.7 copy-done.5
  12.3 19.4 %attention.1 = (bf16[1,2048,256]{2,1,0:T(8,128)(2,1)}, bf16[256,2048]{1,0:T(8,128)(2,1)S(1)}) custom-call(f32[1,4]{1,0:T(1,128)S(1)} %copy-done.2, s32[1,4]{1,0:T(1,128)S(1)} %copy-done.3, s32[1,16]{1,0:T(1,128)S(1)} %copy-done.4, s32[1,16]{1,0:T(1,128)S(1)} %copy-done.5, bf16[1,2048,256]{2,1,0:T(8,128)(2,1)S(1)} %copy-done, ...), custom_call_target="tpu_custom_call" | custom-call | flops 10000000000 | bytes 8388608 | tf_op jit(solution)/shard_map/attention/pallas_call | solution.py:127
  31.7 0.0 copy-start.6
  31.8 0.2 collective-permute-start
  32.0 13.6 %collective-permute-done = bf16[128,2048]{1,0:T(8,128)(2,1)S(1)} collective-permute-done((bf16[128,2048]{1,0:T(8,128)(2,1)S(1)}, bf16[128,2048]{1,0:T(8,128)(2,1)S(1)}, u32[]{:S(2)}, u32[]{:S(2)}) %collective-permute-start) | collective-permute-done | bytes 524320 | tf_op jit(solution)/shard_map/ppermute | solution.py:159
  45.6 0.1 add_convert_fusion
  45.7 0.1 collective-permute-start.1
  45.8 1.5 collective-permute-done.1
  47.3 0.8 add_convert_fusion.1
  48.1 0.0 all-gather.2.cloned.1.call-update
  48.1 0.0 reduce-scatter.2.cloned.1.call-start
  48.2 0.0 copy-done.6
  48.2 0.7 copy.10
  48.9 19.3 %all_to_all.19 = bf16[128,16,256]{0,2,1:T(8,128)(2,1)S(1)} all-to-all(bf16[128,16,256]{0,2,1:T(8,128)(2,1)S(1)} %bitcast.7), channel_id=1, replica_groups=mesh['dp'=16,'tp'=16] {'tp'}, dimensions={1} | all-to-all | bytes 2097152 | tf_op jit(solution)/shard_map/all_to_all | solution.py:152
  68.2 0.5 copy.11
  68.7 24.6 %all-gather.2.cloned.1.call-done = bf16[1024,2048]{1,0:T(8,128)(2,1)} async-done(((bf16[64,2048]{1,0:T(8,128)(2,1)}), bf16[1024,2048]{1,0:T(8,128)(2,1)}) %all-gather.2.cloned.1.call-update) | async-done | bytes 4194320 | tf_op jit(solution)/shard_map/all_gather | solution.py:161
  93.3 4.4 %fusion = f32[1024,256]{1,0:T(8,128)} fusion(bf16[1024,2048]{1,0:T(8,128)(2,1)} %all-gather.2.cloned.1.call-done, bf16[2048,256]{1,0:T(8,128)(2,1)S(1)} %bitcast.8), kind=kOutput, calls=%fused_computation.4 | convolution fusion | flops 1073741824 | bytes 6291456 | tf_op jit(solution)/shard_map/dot_general | solution.py:162
  97.7 0.0 reduce-scatter.2.cloned.1.call-update
  97.7 89.7 %reduce-scatter.2.cloned.1.call-done = f32[64,256]{1,0:T(8,128)} async-done(((f32[1024,256]{1,0:T(8,128)}), f32[64,256]{1,0:T(8,128)}) %reduce-scatter.2.cloned.1.call-update) | async-done | bytes 65552 | tf_op jit(solution)/shard_map/reduce_scatter | solution.py:163
  187.4 6.2 %collective-permute-start.2 = (f32[64,256]{1,0:T(8,128)}, f32[64,256]{1,0:T(8,128)S(1)}, u32[]{:S(2)}, u32[]{:S(2)}) collective-permute-start(f32[64,256]{1,0:T(8,128)} %reduce-scatter.2.cloned.1.call-done), channel_id=1, source_target_pairs={{0,0},{1,16},{2,32},{3,48},{4,64},{5,80},{6,96},{7,112},{8,128},{9... | collective-permute-start | bytes 196616 | tf_op jit(solution)/shard_map/ppermute | solution.py:164
  193.6 7.9 %collective-permute-done.2 = f32[64,256]{1,0:T(8,128)S(1)} collective-permute-done((f32[64,256]{1,0:T(8,128)}, f32[64,256]{1,0:T(8,128)S(1)}, u32[]{:S(2)}, u32[]{:S(2)}) %collective-permute-start.2) | collective-permute-done | bytes 65568 | tf_op jit(solution)/shard_map/ppermute | solution.py:164
  201.6 0.6 copy.13
  (4 shorter events, 0.1 us)
Async XLA Ops:
  7.2 86.1 %all-gather.2.cloned.1.call-start = ((), (), s32[]{:S(2)}) async-start(), calls=%async_computation.2 | async-start | bytes 4456448 | tf_op jit(solution)/shard_map/all_gather | solution.py:161
  7.2 1.2 copy-start
  8.5 1.2 copy-start.1
  9.7 0.7 copy-start.2
  10.4 0.7 copy-start.3
  11.0 0.7 copy-start.4
  11.7 0.7 copy-start.5
  31.7 16.5 %copy-start.6 = (bf16[1,128,4096]{2,1,0:T(8,128)(2,1)S(1)}, bf16[1,128,4096]{2,1,0:T(8,128)(2,1)}, u32[]{:S(2)}) copy-start(bf16[1,128,4096]{2,1,0:T(8,128)(2,1)} %param.8) | copy-start | bytes 3145732
  31.8 13.8 %collective-permute-start = (bf16[128,2048]{1,0:T(8,128)(2,1)S(1)}, bf16[128,2048]{1,0:T(8,128)(2,1)S(1)}, u32[]{:S(2)}, u32[]{:S(2)}) collective-permute-start(bf16[128,2048]{1,0:T(8,128)(2,1)S(1)} %constant_dynamic-slice_fusion.1), channel_id=1, source_target_pairs={{0,2},{1,3},{2,0},{3,1},{4,6},{5,7},{6,4},{7,5},{8,10},{9,11},{10,... | collective-permute-start | bytes 1572872 | tf_op jit(solution)/shard_map/ppermute | solution.py:159
  45.7 1.6 collective-permute-start.1
  48.1 139.3 %reduce-scatter.2.cloned.1.call-start = ((), (), s32[]{:S(2)}) async-start(), calls=%async_computation.3 | async-start | bytes 1114112 | tf_op jit(solution)/shard_map/reduce_scatter | solution.py:163
  187.4 14.2 %collective-permute-start.2 = (f32[64,256]{1,0:T(8,128)}, f32[64,256]{1,0:T(8,128)S(1)}, u32[]{:S(2)}, u32[]{:S(2)}) collective-permute-start(f32[64,256]{1,0:T(8,128)} %reduce-scatter.2.cloned.1.call-done), channel_id=1, source_target_pairs={{0,0},{1,16},{2,32},{3,48},{4,64},{5,80},{6,96},{7,112},{8,128},{9... | collective-permute-start | bytes 196616 | tf_op jit(solution)/shard_map/ppermute | solution.py:164
Sparse Core Ops, SparseCore 0:
  48.3 44.9 all-gather.1
  97.9 89.5 reduce-scatter.1

commit v2 on v1

--- a/solution.py
+++ b/solution.py
@@ -146,23 +146,226 @@
     )(ratio, pair, item, image, queries, out_grad, key_values)
 
 
+CHUNKS = 4
+MESH = pl.DeviceIdType.MESH
+
+
+def exchange_kernel(kvt, x_own, x1, x2, x3, x4, x5, x6, x7, out_ref,
+                    own, core_in, part, z_in, heads, xs, stage, landed,
+                    core_s, core_r, z_s, z_r, right_s, right_r, left_s, left_r,
+                    fr_s, fr_r, fl_s, fl_r, xs_s, xs_r, load_sem, x_sem, out_s, out_r):
+    dp = lax.axis_index("dp")
+    tp = lax.axis_index("tp")
+    x = tp // 4
+    zl = tp // 2 % 2
+    c = tp % 2
+    place = tp // 2
+    half = 2 * HD // 2
+    rows = half // CHUNKS
+    length = heads.shape[2]
+    cols = xs.shape[3]
+    sibling = x * 4 + zl * 2 + (1 - c)
+    across = x * 4 + (1 - zl) * 2 + c
+    right = lax.rem(x + 1, 4) * 4 + zl * 2 + c
+    left = lax.rem(x + 3, 4) * 4 + zl * 2 + c
+
+    load = pltpu.make_async_copy(kvt.at[pl.ds(pl.multiple_of(c * half, half), half)], own, load_sem)
+    load.start()
+    x_loads = []
+    sources = (x_own, x1, x2, x3, x4, x5, x6, x7)
+    for i, src in enumerate(sources):
+        dx, dz = i // 2, i % 2
+        j = lax.rem(x + 4 - dx, 4) * 2 + lax.rem(zl + dz, 2)
+        if i == 0:
+            src = src.at[:, pl.ds(pl.multiple_of(place * cols, cols), cols)]
+        cp = pltpu.make_async_copy(src, xs.at[j, c], x_sem.at[i])
+        cp.start()
+        x_loads.append(cp)
+
+    barrier = pltpu.get_barrier_semaphore()
+    for partner in (sibling, across, right, left):
+        pl.semaphore_signal(barrier, 1, device_id=(dp, partner), device_id_type=MESH)
+
+    def dest(k, h, e):
+        return place * 2 + e, h * 4 + c * 2 + k // 2
+
+    def greet_dest(i, n):
+        u, h, e = i // 8, i // 2 % 4, i % 2
+        d, t = dest(u * 2, h, e)
+        other = jnp.logical_or(d != dp, t != tp)
+
+        @pl.when(other)
+        def _():
+            pl.semaphore_signal(barrier, 1, device_id=(d, t), device_id_type=MESH)
+        return n + jnp.where(other, 1, 0)
+
+    src_tp = (dp // 4) * 4 + (dp % 4 // 2) * 2 + zl
+
+    def greet_source(i, n):
+        other = jnp.logical_or(i != dp, src_tp != tp)
+
+        @pl.when(other)
+        def _():
+            pl.semaphore_signal(barrier, 1, device_id=(i, src_tp), device_id_type=MESH)
+        return n + jnp.where(other, 1, 0)
+
+    n = lax.fori_loop(0, 16, greet_dest, jnp.int32(4))
+    n = lax.fori_loop(0, 16, greet_source, n)
+    pl.semaphore_wait(barrier, n)
+
+    def remote(src, dst, ss, rs, t):
+        return pltpu.make_async_remote_copy(src_ref=src, dst_ref=dst, send_sem=ss, recv_sem=rs,
+                                            device_id=(dp, t), device_id_type=MESH)
+
+    def cut(k):
+        return pl.ds(k * rows, rows)
+
+    core = []
+    for k in range(CHUNKS):
+        base = pl.multiple_of((1 - c) * half, half)
+        cp = remote(kvt.at[pl.ds(base + k * rows, rows)], core_in.at[cut(k)], core_s.at[k], core_r.at[k], sibling)
+        cp.start()
+        core.append(cp)
+    for cp in x_loads:
+        cp.wait()
+    x_send = remote(xs.at[:, c], xs.at[:, c], xs_s, xs_r, sibling)
+    x_send.start()
+    load.wait()
+
+    zc, rc, lc, frc, flc = [], [], [], [], []
+
+    def reduce_core(k):
+        core[k].wait_recv()
+        part[cut(k)] = (own[cut(k)].astype(jnp.float32) + core_in[cut(k)].astype(jnp.float32)).astype(jnp.bfloat16)
+        cp = remote(part.at[cut(k)], z_in.at[cut(k)], z_s.at[k], z_r.at[k], across)
+        cp.start()
+        zc.append(cp)
+
+    def reduce_z(k):
+        zc[k].wait_recv()
+        heads[x, cut(k)] = (part[cut(k)].astype(jnp.float32) + z_in[cut(k)].astype(jnp.float32)).astype(jnp.bfloat16)
+        here = heads.at[x, cut(k)]
+        for lst, ss, rs, t in ((rc, right_s, right_r, right), (lc, left_s, left_r, left)):
+            cp = remote(here, here, ss.at[k], rs.at[k], t)
+            cp.start()
+            lst.append(cp)
+
+    def forward(k):
+        rc[k].wait_recv()
+        a = heads.at[lax.rem(x + 3, 4), cut(k), pl.ds(0, length // 2)]
+        cp = remote(a, a, fr_s.at[k], fr_r.at[k], right)
+        cp.start()
+        frc.append(cp)
+        lc[k].wait_recv()
+        b = heads.at[lax.rem(x + 1, 4), cut(k), pl.ds(length // 2, length // 2)]
+        cp = remote(b, b, fl_s.at[k], fl_r.at[k], left)
+        cp.start()
+        flc.append(cp)
+
+    def out_copy(k, i, d, t):
+        h, e = i // 2, i % 2
+        return pltpu.make_async_remote_copy(
+            src_ref=stage.at[k, h, e], dst_ref=landed.at[dp, k % 2], send_sem=out_s.at[k * 8 + i],
+            recv_sem=out_r.at[dp, k % 2], device_id=(d, t), device_id_type=MESH)
+
+    def multiply(k):
+        frc[k].wait_recv()
+        flc[k].wait_recv()
+        if k == 0:
+            x_send.wait_recv()
+        lhs = heads[:, k * rows:(k + 1) * rows, :].reshape(4 * rows, length)
+        res = jnp.dot(lhs, xs[...].reshape(length, cols), preferred_element_type=jnp.float32)
+        res = res.astype(jnp.bfloat16).reshape(4, rows, cols)
+        for e in range(2):
+            stage[k, :, e] = res[:, :, e * (cols // 2):(e + 1) * (cols // 2)]
+
+        def send(i, carry):
+            d, t = dest(k, i // 2, i % 2)
+            other = jnp.logical_or(d != dp, t != tp)
+
+            @pl.when(other)
+            def _():
+                out_copy(k, i, d, t).start()
+
+            @pl.when(jnp.logical_not(other))
+            def _():
+                pltpu.make_async_copy(stage.at[k, i // 2, i % 2], landed.at[dp, k % 2], out_r.at[dp, k % 2]).start()
+            return carry
+        lax.fori_loop(0, 8, send, 0)
+
+    for step in range(CHUNKS + 3):
+        if step < CHUNKS:
+            reduce_core(step)
+        if 0 <= step - 1 < CHUNKS:
+            reduce_z(step - 1)
+        if 0 <= step - 2 < CHUNKS:
+            forward(step - 2)
+        if 0 <= step - 3 < CHUNKS:
+            multiply(step - 3)
+
+    def collect(i, total):
+        new = []
+        for p in range(2):
+            pltpu.make_async_copy(landed.at[i, p], landed.at[i, p], out_r.at[i, p]).wait()
+            new.append(total[p] + landed[i, p].astype(jnp.float32))
+        return tuple(new)
+
+    zero = jnp.zeros((rows, cols // 2), jnp.float32)
+    top, bottom = lax.fori_loop(0, 16, collect, (zero, zero))
+    out_ref[:rows] = top
+    out_ref[rows:] = bottom
+
+    for group in (core, zc, rc, lc, frc, flc, [x_send]):
+        for cp in group:
+            cp.wait_send()
+
+    def drain(j, carry):
+        k, i = j // 8, j % 8
+        d, t = dest(k, i // 2, i % 2)
+
+        @pl.when(jnp.logical_or(d != dp, t != tp))
+        def _():
+            out_copy(k, i, d, t).wait_send()
+        return carry
+    lax.fori_loop(0, 8 * CHUNKS, drain, 0)
+
+
+def exchange(kvt, x_own, others):
+    length = kvt.shape[1]
+    cols = others[0].shape[1]
+    half = HD
+    rows = half // CHUNKS
+    sem = pltpu.SemaphoreType.DMA
+    bf = jnp.bfloat16
+    return pl.pallas_call(
+        exchange_kernel,
+        out_shape=jax.ShapeDtypeStruct((2 * rows, cols // 2), jnp.float32),
+        in_specs=[pl.BlockSpec(memory_space=pl.ANY)] * 9,
+        out_specs=pl.BlockSpec(memory_space=pltpu.VMEM),
+        scratch_shapes=[
+            pltpu.VMEM((half, length), bf), pltpu.VMEM((half, length), bf),
+            pltpu.VMEM((half, length), bf), pltpu.VMEM((half, length), bf),
+            pltpu.VMEM((4, half, length), bf), pltpu.VMEM((8, 2, TILE, cols), bf),
+            pltpu.VMEM((CHUNKS, 4, 2, rows, cols // 2), bf), pltpu.VMEM((16, 2, rows, cols // 2), bf),
+        ] + [sem((CHUNKS,))] * 12 + [sem, sem, sem, sem((8,)), sem((8 * CHUNKS,)), sem((16, 2))],
+        compiler_params=pltpu.CompilerParams(collective_id=0, has_side_effects=True, vmem_limit_bytes=48 << 20),
+        cost_estimate=pl.CostEstimate(flops=10**9, bytes_accessed=8 << 20, transcendentals=0),
+        name="exchange",
+    )(kvt, x_own, *others)
+
+
 def local(input_rows, queries, key_values, out_grad, item_logratio, pair_ids, tile_item, tile_image):
-    tp = lax.axis_size("tp")
     t = lax.axis_index("tp")
-    xc = lax.all_to_all(input_rows[0], "tp", 1, 0, tiled=True)
-    dq, part = attention(queries, out_grad, key_values, item_logratio, pair_ids, tile_item, tile_image)
-    for bit in (1, 0):
-        half = part.shape[0] // 2
-        mine = t // 2**bit % 2
-        kept = lax.dynamic_slice_in_dim(part, mine * half, half, 0)
-        sent = lax.dynamic_slice_in_dim(part, (1 - mine) * half, half, 0)
-        got = lax.ppermute(sent, "tp", [(i, i ^ 1 << bit) for i in range(tp)])
-        part = (kept.astype(jnp.float32) + got.astype(jnp.float32)).astype(jnp.bfloat16)
-    whole = lax.all_gather(part, "tp", axis=0, tiled=True)
-    wt = jnp.dot(whole, xc, preferred_element_type=jnp.float32)
-    wt = lax.psum_scatter(wt, "dp", scatter_dimension=0, tiled=True)
-    wt = lax.ppermute(wt, ("dp", "tp"), [(a * tp + b, b * tp + a) for a in range(tp) for b in range(tp)])
-    return dq, wt.T
+    rows = input_rows[0]
+    cols = rows.shape[1] // 8
+    others = []
+    for i in range(1, 8):
+        dx, dz = i // 2, i % 2
+        to = (t // 4 + dx) % 4 * 2 + (t // 2 + dz) % 2
+        pairs = [(a, (a // 4 + dx) % 4 * 4 + (a // 2 + dz) % 2 * 2 + a % 2) for a in range(16)]
+        others.append(lax.ppermute(lax.dynamic_slice_in_dim(rows, to * cols, cols, 1), "tp", pairs))
+    dq, kvt = attention(queries, out_grad, key_values, item_logratio, pair_ids, tile_item, tile_image)
+    return dq, exchange(kvt, rows, others).T
 
 
 def solution(mesh):

time: 209 us -> 94.1 us (0.45)
  the two profiles are of different devices: /device:TPU:36 before, /device:TPU:1 now
where the time goes in v2:
time: 94.1 us; the launch traced here: 93.7 us
  Pallas kernels  72.6 us (77%)
  starting transfers between devices  11.1 us (12%)
  local copies, waits for them, and re-layouts  7.04 us (7%)
  waiting for transfers between devices  2.09 us (2%)
    pallas_call x1, Pallas kernels, exchange(): pl.pallas_call(exchange_kernel, out_shape=jax.ShapeDtypeStruct((2 * rows,...  55.1 us
    pallas_call x1, Pallas kernels, attention(): pl.pallas_call(attention_kernel, out_shape=[jax.ShapeDtypeStruct(queries....  17.5 us
    ppermute x7, starting transfers between devices, local(): lax.ppermute(lax.dynamic_slice_in_dim(rows, to * cols, cols, 1), 'tp', pa...  11.1 us
    unnamed x15, local copies, waits for them, and re-layouts  5.7 us
    ppermute x7, waiting for transfers between devices, local(): lax.ppermute(lax.dynamic_slice_in_dim(rows, to * cols, cols, 1), 'tp', pa...  2.09 us
  transfers between devices with their start and end apart: 7, of which 1 were waited for; matrix products, arithmetic and copies ran while one was open for 0% of the time, Pallas kernels for 19%

profile of v2, /device:TPU:1, one launch (start us, length us, event | category | flops | bytes accessed | tf_op | source)
XLA Modules:
  0.0 93.7 jit_solution(14165515630026418354)
XLA Ops:
  0.8 1.3 %dynamic-slice_bitcast_fusion = (bf16[128,512]{1,0:T(8,128)(2,1)S(1)}, bf16[128,512]{1,0:T(8,128)(2,1)S(1)}, bf16[128,512]{1,0:T(8,128)(2,1)S(1)}, bf16[128,512]...) fusion(bf16[1,128,4096]{2,1,0:T(8,128)(2,1)} %param.8, ...), kind=kLoop, calls=%fused_computation | loop fusion | bytes 1835036 | tf_op jit(solution)/shard_map/dynamic_slice | solution.py:366
  2.1 4.7 %collective-permute-start.6 = (bf16[128,512]{1,0:T(8,128)(2,1)S(1)}, bf16[128,512]{1,0:T(8,128)(2,1)S(1)}, u32[]{:S(2)}, u32[]{:S(2)}) collective-permute-start(bf16[128,512]{1,0:T(8,128)(2,1)S(1)} %get-tuple-element.6), channel_id=1, source_target_pairs={{0,14},{1,15},{2,12},{3,13},{4,2},{5,3},{6,0},{7,1},{8,6},{9,7},{1... | collective-permute-start | bytes 393224 | tf_op jit(solution)/shard_map/ppermute | solution.py:366
  6.9 0.4 collective-permute-start.4
  7.2 2.2 %collective-permute-start.3 = (bf16[128,512]{1,0:T(8,128)(2,1)S(1)}, bf16[128,512]{1,0:T(8,128)(2,1)S(1)}, u32[]{:S(2)}, u32[]{:S(2)}) collective-permute-start(bf16[128,512]{1,0:T(8,128)(2,1)S(1)} %get-tuple-element.8), channel_id=1, source_target_pairs={{0,8},{1,9},{2,10},{3,11},{4,12},{5,13},{6,14},{7,15},{8,0},{9,1},... | collective-permute-start | bytes 393224 | tf_op jit(solution)/shard_map/ppermute | solution.py:366
  9.4 0.3 collective-permute-start.2
  9.7 1.2 %collective-permute-start.1 = (bf16[128,512]{1,0:T(8,128)(2,1)S(1)}, bf16[128,512]{1,0:T(8,128)(2,1)S(1)}, u32[]{:S(2)}, u32[]{:S(2)}) collective-permute-start(bf16[128,512]{1,0:T(8,128)(2,1)S(1)} %get-tuple-element.10), channel_id=1, source_target_pairs={{0,4},{1,5},{2,6},{3,7},{4,8},{5,9},{6,10},{7,11},{8,12},{9,13},{1... | collective-permute-start | bytes 393224 | tf_op jit(solution)/shard_map/ppermute | solution.py:366
  10.9 0.0 collective-permute-done.6.x7
  10.9 0.2 collective-permute-start
  11.1 2.1 %collective-permute-done.4.x5 = bf16[128,512]{1,0:T(8,128)(2,1)S(1)} collective-permute-done((bf16[128,512]{1,0:T(8,128)(2,1)S(1)}, bf16[128,512]{1,0:T(8,128)(2,1)S(1)}, u32[]{:S(2)}, u32[]{:S(2)}) %collective-permute-start.4) | collective-permute-done | bytes 131104 | tf_op jit(solution)/shard_map/ppermute | solution.py:366
  13.2 0.0 copy-start
  13.2 2.1 %collective-permute-start.5 = (bf16[128,512]{1,0:T(8,128)(2,1)S(1)}, bf16[128,512]{1,0:T(8,128)(2,1)S(1)}, u32[]{:S(2)}, u32[]{:S(2)}) collective-permute-start(bf16[128,512]{1,0:T(8,128)(2,1)S(1)} %get-tuple-element.12), channel_id=1, source_target_pairs={{0,12},{1,13},{2,14},{3,15},{4,0},{5,1},{6,2},{7,3},{8,4},{9,5},{1... | collective-permute-start | bytes 393224 | tf_op jit(solution)/shard_map/ppermute | solution.py:366
  15.3 0.0 copy-start.1
  15.3 1.2 %copy-done.1 = bf16[1,2048,256]{2,1,0:T(8,128)(2,1)S(1)} copy-done((bf16[1,2048,256]{2,1,0:T(8,128)(2,1)S(1)}, bf16[1,2048,256]{2,1,0:T(8,128)(2,1)}, u32[]{:S(2)}) %copy-start.1) | copy-done | bytes 1048600
  16.5 0.0 copy-start.2
  16.5 1.2 %copy-done.2 = bf16[1,2048,256]{2,1,0:T(8,128)(2,1)S(1)} copy-done((bf16[1,2048,256]{2,1,0:T(8,128)(2,1)S(1)}, bf16[1,2048,256]{2,1,0:T(8,128)(2,1)}, u32[]{:S(2)}) %copy-start.2) | copy-done | bytes 1048600
  17.8 0.0 copy-start.3
  17.8 0.7 copy-done.3
  18.4 0.0 copy-start.4
  18.4 0.7 copy-done.4
  19.1 0.0 copy-start.5
  19.1 0.7 copy-done.5
  19.7 0.0 copy-start.6
  19.7 0.7 copy-done.6
  20.4 17.5 %attention.1 = (bf16[1,2048,256]{2,1,0:T(8,128)(2,1)}, bf16[256,2048]{1,0:T(8,128)(2,1)S(1)}) custom-call(f32[1,4]{1,0:T(1,128)S(1)} %copy-done.3, s32[1,4]{1,0:T(1,128)S(1)} %copy-done.4, s32[1,16]{1,0:T(1,128)S(1)} %copy-done.5, s32[1,16]{1,0:T(1,128)S(1)} %copy-done.6, bf16[1,2048,256]{2,1,0:T(8,128)(2,1)S(1)} %copy-done.1, ...), custom_call_target="tpu_custom_call" | custom-call | flops 10000000000 | bytes 8388608 | tf_op jit(solution)/shard_map/attention/pallas_call | solution.py:127
  37.9 0.0 collective-permute-done.3.x4
  37.9 0.0 collective-permute-done.2.x3
  37.9 0.0 collective-permute-done.1.x2
  38.0 0.0 collective-permute-done.x1
  38.0 0.0 collective-permute-done.5.x6
  38.0 0.0 copy-done
  38.0 55.1 %exchange.1 = f32[64,256]{1,0:T(8,128)S(1)} custom-call(bf16[256,2048]{1,0:T(8,128)(2,1)S(1)} %get-tuple-element.5.kvt, bf16[128,4096]{1,0:T(8,128)(2,1)S(1)} %bitcast.16, bf16[128,512]{1,0:T(8,128)(2,1)S(1)} %collective-permute-done.x1, bf16[128,512]{1,0:T(8,128)(2,1)S(1)} %collective-permute-done.1.x2, bf16[128,512]{1,0:T(8,128)(2,1)S(1)} %collective-permute-done.2.x3, ...), custom_call_target="tpu_custom_call" | custom-call | flops 1000000000 | bytes 8388608 | tf_op jit(solution)/shard_map/exchange/pallas_call | solution.py:340
  93.1 0.6 copy.11
Async XLA Ops:
  2.1 8.8 %collective-permute-start.6 = (bf16[128,512]{1,0:T(8,128)(2,1)S(1)}, bf16[128,512]{1,0:T(8,128)(2,1)S(1)}, u32[]{:S(2)}, u32[]{:S(2)}) collective-permute-start(bf16[128,512]{1,0:T(8,128)(2,1)S(1)} %get-tuple-element.6), channel_id=1, source_target_pairs={{0,14},{1,15},{2,12},{3,13},{4,2},{5,3},{6,0},{7,1},{8,6},{9,7},{1... | collective-permute-start | bytes 393224 | tf_op jit(solution)/shard_map/ppermute | solution.py:366
  6.9 6.3 %collective-permute-start.4 = (bf16[128,512]{1,0:T(8,128)(2,1)S(1)}, bf16[128,512]{1,0:T(8,128)(2,1)S(1)}, u32[]{:S(2)}, u32[]{:S(2)}) collective-permute-start(bf16[128,512]{1,0:T(8,128)(2,1)S(1)} %get-tuple-element.7), channel_id=1, source_target_pairs={{0,10},{1,11},{2,8},{3,9},{4,14},{5,15},{6,12},{7,13},{8,2},{9,3},... | collective-permute-start | bytes 393224 | tf_op jit(solution)/shard_map/ppermute | solution.py:366
  7.2 30.7 %collective-permute-start.3 = (bf16[128,512]{1,0:T(8,128)(2,1)S(1)}, bf16[128,512]{1,0:T(8,128)(2,1)S(1)}, u32[]{:S(2)}, u32[]{:S(2)}) collective-permute-start(bf16[128,512]{1,0:T(8,128)(2,1)S(1)} %get-tuple-element.8), channel_id=1, source_target_pairs={{0,8},{1,9},{2,10},{3,11},{4,12},{5,13},{6,14},{7,15},{8,0},{9,1},... | collective-permute-start | bytes 393224 | tf_op jit(solution)/shard_map/ppermute | solution.py:366
  9.4 28.6 %collective-permute-start.2 = (bf16[128,512]{1,0:T(8,128)(2,1)S(1)}, bf16[128,512]{1,0:T(8,128)(2,1)S(1)}, u32[]{:S(2)}, u32[]{:S(2)}) collective-permute-start(bf16[128,512]{1,0:T(8,128)(2,1)S(1)} %get-tuple-element.9), channel_id=1, source_target_pairs={{0,6},{1,7},{2,4},{3,5},{4,10},{5,11},{6,8},{7,9},{8,14},{9,15},{1... | collective-permute-start | bytes 393224 | tf_op jit(solution)/shard_map/ppermute | solution.py:366
  9.7 28.2 %collective-permute-start.1 = (bf16[128,512]{1,0:T(8,128)(2,1)S(1)}, bf16[128,512]{1,0:T(8,128)(2,1)S(1)}, u32[]{:S(2)}, u32[]{:S(2)}) collective-permute-start(bf16[128,512]{1,0:T(8,128)(2,1)S(1)} %get-tuple-element.10), channel_id=1, source_target_pairs={{0,4},{1,5},{2,6},{3,7},{4,8},{5,9},{6,10},{7,11},{8,12},{9,13},{1... | collective-permute-start | bytes 393224 | tf_op jit(solution)/shard_map/ppermute | solution.py:366
  10.9 27.0 %collective-permute-start = (bf16[128,512]{1,0:T(8,128)(2,1)S(1)}, bf16[128,512]{1,0:T(8,128)(2,1)S(1)}, u32[]{:S(2)}, u32[]{:S(2)}) collective-permute-start(bf16[128,512]{1,0:T(8,128)(2,1)S(1)} %get-tuple-element.11), channel_id=1, source_target_pairs={{0,2},{1,3},{2,0},{3,1},{4,6},{5,7},{6,4},{7,5},{8,10},{9,11},{10,... | collective-permute-start | bytes 393224 | tf_op jit(solution)/shard_map/ppermute | solution.py:366
  13.2 24.8 %copy-start = (bf16[1,128,4096]{2,1,0:T(8,128)(2,1)S(1)}, bf16[1,128,4096]{2,1,0:T(8,128)(2,1)}, u32[]{:S(2)}) copy-start(bf16[1,128,4096]{2,1,0:T(8,128)(2,1)} %param.8) | copy-start | bytes 3145732
  13.2 24.8 %collective-permute-start.5 = (bf16[128,512]{1,0:T(8,128)(2,1)S(1)}, bf16[128,512]{1,0:T(8,128)(2,1)S(1)}, u32[]{:S(2)}, u32[]{:S(2)}) collective-permute-start(bf16[128,512]{1,0:T(8,128)(2,1)S(1)} %get-tuple-element.12), channel_id=1, source_target_pairs={{0,12},{1,13},{2,14},{3,15},{4,0},{5,1},{6,2},{7,3},{8,4},{9,5},{1... | collective-permute-start | bytes 393224 | tf_op jit(solution)/shard_map/ppermute | solution.py:366
  15.3 1.2 %copy-start.1 = (bf16[1,2048,256]{2,1,0:T(8,128)(2,1)S(1)}, bf16[1,2048,256]{2,1,0:T(8,128)(2,1)}, u32[]{:S(2)}) copy-start(bf16[1,2048,256]{2,1,0:T(8,128)(2,1)} %q_ref.1) | copy-start | bytes 3145732
  16.5 1.2 %copy-start.2 = (bf16[1,2048,256]{2,1,0:T(8,128)(2,1)S(1)}, bf16[1,2048,256]{2,1,0:T(8,128)(2,1)}, u32[]{:S(2)}) copy-start(bf16[1,2048,256]{2,1,0:T(8,128)(2,1)} %og_ref.1) | copy-start | bytes 3145732
  17.8 0.7 copy-start.3
  18.4 0.7 copy-start.4
  19.1 0.7 copy-start.5
  19.7 0.7 copy-start.6

commit v3 on v1

v3 whole, which is shorter than its diff:
```python
import functools, math
import jax, jax.numpy as jnp
from jax import lax
from jax.experimental import pallas as pl
from jax.experimental.pallas import tpu as pltpu

from jax.sharding import PartitionSpec as P

KVH = 4; HD = 128; TILE = 128; BETA = 0.1
MASKED = -1e30
LOG2E = 1.4426950408889634

def attention_kernel(ratio_h, pair_h, item_h, image_h, q_hbm, og_hbm, kv_hbm, dq_hbm, kvt_ref,
                     kv, q_ref, og_ref, dq_ref, s0, s1, dp0, dp1, acc, ratio, pair, item, image,
                     lo_s, hi_s, z_s, small_sem, big_sem, dq_sem):
    group = lax.axis_size("tp") // KVH
    g = lax.axis_index("tp") // group
    nt = item.shape[1]
    items = ratio.shape[1]
    small = [pltpu.make_async_copy(a, b, small_sem.at[i])
             for i, (a, b) in enumerate(((ratio_h, ratio), (pair_h, pair), (item_h, item), (image_h, image)))]
    for cp in small:
        cp.start()
    big = [pltpu.make_async_copy(kv_hbm.at[0, :, pl.ds(pl.multiple_of(g * 2 * HD, 2 * HD), 2 * HD)], kv, big_sem.at[0]),
           pltpu.make_async_copy(q_hbm.at[0], q_ref, big_sem.at[1]),
           pltpu.make_async_copy(og_hbm.at[0], og_ref, big_sem.at[2])]
    for cp in big:
        cp.start()
    inv_root = 1.0 / math.sqrt(HD)
    c2 = inv_root * LOG2E
    W = 2 * TILE
    acc[...] = jnp.zeros_like(acc)
    for cp in small:
        cp.wait()
    lo_s[0] = 0
    for i in range(1, nt):
        lo_s[i] = jnp.where(item[0, i] == item[0, i - 1], lo_s[i - 1], i)
    hi_s[nt - 1] = nt - 1
    for i in reversed(range(nt - 1)):
        same = (image[0, i] > 0) & (image[0, i] == image[0, i + 1]) & (item[0, i] == item[0, i + 1])
        hi_s[i] = jnp.where(same, hi_s[i + 1], i)
    for a in range(items):
        other = jnp.float32(0.0)
        p = jnp.float32(1.0)
        for b in range(items):
            if b != a:
                same = pair[0, a] == pair[0, b]
                other = other + jnp.where(same, ratio[0, b], 0.0)
                if a < b:
                    p = jnp.where(same, -1.0, p)
        z_s[a] = BETA * p * (other - ratio[0, a])
        z_s[items + a] = p
    for cp in big:
        cp.wait()

    def block(I, n, spare, s_scr, dp_scr):
        lo = lo_s[I]
        hi = hi_s[I]
        img = image[0, I]
        it = item[0, I]
        r0 = pl.multiple_of(I * TILE, TILE)
        st = pl.multiple_of(jnp.clip(hi + 1 - 2 * n, 0, nt - 2 * n) * TILE, TILE)
        first = lo * TILE - st
        v = {}

        def stage1():
            qi = q_ref[pl.ds(r0, TILE), :]
            q2 = jnp.concatenate([qi[:, :HD], qi[:, HD:]], axis=0)
            coef = z_s[items + it] / (1.0 + jnp.exp(jnp.full((8, HD), z_s[it], jnp.float32)))
            coef = jnp.concatenate([coef[:1], coef[:1]], axis=1)
            wi = (og_ref[pl.ds(r0, TILE), :].astype(jnp.float32) * coef).astype(jnp.bfloat16)
            w2 = jnp.concatenate([wi[:, :HD], wi[:, HD:]], axis=0)
            v["q2t"] = q2.T
            v["w2t"] = w2.T
            row = lax.broadcasted_iota(jnp.int32, (TILE, 1), 0)
            row = jnp.concatenate([row, row], axis=0)
            last = jnp.where(img > 0, jnp.full((2 * TILE, 1), (hi + 1) * TILE - 1 - st), r0 - st + row)
            m = None
            for ch in range(n):
                rows = pl.ds(st + ch * W, W)
                s = lax.dot_general(q2, kv[rows, :HD], (((1,), (1,)), ((), ())), preferred_element_type=jnp.float32)
                if ch <= spare or ch == n - 1:
                    col = lax.broadcasted_iota(jnp.int32, (1, W), 1) + ch * W
                    ok = (col <= last) & (col >= first)
                    s = jnp.where(ok, s, MASKED)
                s_scr[:, ch * W:(ch + 1) * W] = s
                mm = jnp.maximum(s[:, :HD], s[:, HD:])
                m = mm if m is None else jnp.maximum(m, mm)
                dp_scr[:, ch * W:(ch + 1) * W] = lax.dot_general(
                    w2, kv[rows, HD:], (((1,), (1,)), ((), ())), preferred_element_type=jnp.float32)
            v["m"] = jnp.max(m, axis=1, keepdims=True) * c2

        def stage2():
            mr = v["m"]
            l = r = None
            for ch in range(n):
                cols = slice(ch * W, (ch + 1) * W)
                p = jnp.exp2(s_scr[:, cols] * c2 - mr)
                s_scr[:, cols] = p
                pd = p * dp_scr[:, cols]
                ll = p[:, :HD] + p[:, HD:]
                rr = pd[:, :HD] + pd[:, HD:]
                l = ll if l is None else l + ll
                r = rr if r is None else r + rr
            v["inv"] = 1.0 / jnp.sum(l, axis=1, keepdims=True)
            v["rd"] = jnp.sum(r, axis=1, keepdims=True) * v["inv"]

        def stage3():
            inv, rd = v["inv"], v["rd"]
            dq = None
            for ch in range(n):
                rows = pl.ds(st + ch * W, W)
                cols = slice(ch * W, (ch + 1) * W)
                at = s_scr[:, cols] * inv
                ds = (at * (dp_scr[:, cols] - rd)).astype(jnp.bfloat16)
                at = at.astype(jnp.bfloat16)
                d = jnp.dot(ds, kv[rows, :HD], preferred_element_type=jnp.float32)
                dq = d if dq is None else dq + d
                acc[:HD, rows] += jnp.dot(v["q2t"], ds, preferred_element_type=jnp.float32)
                acc[HD:, rows] += jnp.dot(v["w2t"], at, preferred_element_type=jnp.float32)
            dq = (dq * inv_root).astype(jnp.bfloat16)
            dq_ref[pl.ds(r0, TILE), :HD] = dq[:TILE]
            dq_ref[pl.ds(r0, TILE), HD:] = dq[TILE:]

        return stage1, stage2, stage3

    def chunks(I):
        return (hi_s[I] - lo_s[I] + 2) // 2

    def single(I):
        n_here = chunks(I)
        for n in range(1, nt // 2 + 1):
            @pl.when(n_here == n)
            def _():
                for stage in block(I, n, 0, s0, dp0):
                    stage()

    def row_pair(j, carry):
        a = 2 * j
        na, nb = chunks(a), chunks(a + 1)
        most = jnp.maximum(na, nb)
        near = most - jnp.minimum(na, nb) <= 1
        for n in range(1, nt // 2 + 1):
            @pl.when(near & (most == n))
            def _():
                one = block(a, n, 1, s0, dp0)
                two = block(a + 1, n, 1, s1, dp1)
                for f, g2 in zip(one, two):
                    f()
                    g2()

        @pl.when(jnp.logical_not(near))
        def _():
            def each(i, c):
                single(a + i)
                return c
            lax.fori_loop(0, 2, each, 0)
        here = pl.ds(pl.multiple_of(j * 2 * TILE, 2 * TILE), 2 * TILE)
        pltpu.make_async_copy(dq_ref.at[here], dq_hbm.at[0, here], dq_sem.at[j]).start()
        return carry

    lax.fori_loop(0, nt // 2, row_pair, 0)
    for i in range(nt // 4):
        for z in range(2):
            frm = slice((2 * i + z) * W, (2 * i + z + 1) * W)
            to = slice(i * W, (i + 1) * W)
            kvt_ref[0, z, :, to] = (acc[:HD, frm] * inv_root).astype(jnp.bfloat16)
            kvt_ref[1, z, :, to] = acc[HD:, frm].astype(jnp.bfloat16)

    def finish(j, carry):
        here = pl.ds(pl.multiple_of(j * 2 * TILE, 2 * TILE), 2 * TILE)
        pltpu.make_async_copy(dq_ref.at[here], dq_hbm.at[0, here], dq_sem.at[j]).wait()
        return carry
    lax.fori_loop(0, nt // 2, finish, 0)


def attention(queries, out_grad, key_values, ratio, pair, item, image):
    L = queries.shape[1]
    nt = L // TILE
    hbm = pl.BlockSpec(memory_space=pl.ANY)
    wide = pltpu.VMEM((2 * TILE, L), jnp.float32)
    low = pltpu.VMEM((L, 2 * HD), jnp.bfloat16)
    return pl.pallas_call(
        attention_kernel,
        out_shape=[jax.ShapeDtypeStruct(queries.shape, jnp.bfloat16),
                   jax.ShapeDtypeStruct((2, 2, HD, L // 2), jnp.bfloat16)],
        in_specs=[hbm] * 7,
        out_specs=[hbm, pl.BlockSpec(memory_space=pltpu.VMEM)],
        scratch_shapes=[low, low, low, low, wide, wide, wide, wide,
            pltpu.VMEM((2 * HD, L), jnp.float32),
            pltpu.SMEM(ratio.shape, jnp.float32),
            pltpu.SMEM(pair.shape, jnp.int32),
            pltpu.SMEM(item.shape, jnp.int32),
            pltpu.SMEM(image.shape, jnp.int32),
            pltpu.SMEM((nt,), jnp.int32),
            pltpu.SMEM((nt,), jnp.int32),
            pltpu.SMEM((2 * ratio.shape[1],), jnp.float32),
            pltpu.SemaphoreType.DMA((4,)), pltpu.SemaphoreType.DMA((3,)), pltpu.SemaphoreType.DMA((nt // 2,)),
        ],
        compiler_params=pltpu.CompilerParams(vmem_limit_bytes=56 << 20),
        cost_estimate=pl.CostEstimate(flops=10 * 10**9, bytes_accessed=8 << 20, transcendentals=0),
        name="attention",
    )(ratio, pair, item, image, queries, out_grad, key_values)


CHUNKS = 4
PARTS = CHUNKS // 2
MESH = pl.DeviceIdType.MESH
F32 = jnp.float32
BF16 = jnp.bfloat16


def exchange_kernel(kvt, x_own, x1, x2, x3, out_ref,
                    own, core_in, part, z_in, heads, xs, prod, y1_out, y1_in, y2_out, y2_in, final, landed,
                    core_s, core_r, z_s, z_r, right_s, right_r, left_s, left_r,
                    fr_s, fr_r, fl_s, fl_r, y1r_s, y1r_r, y1l_s, y1l_r, y2r_s, y2r_r, y2l_s, y2l_r,
                    xs_s, xs_r, load_sem, x_sem, out_s, out_r):
    dp = lax.axis_index("dp")
    tp = lax.axis_index("tp")
    y = dp // 4
    zh = dp % 4
    x = tp // 4
    zl = tp // 2 % 2
    c = tp % 2
    rows, length = z_in.shape[1:]
    cols = xs.shape[3]
    half = length // 2
    mid = cols // 2
    sibling = (dp, x * 4 + zl * 2 + (1 - c))
    across = (dp, x * 4 + (1 - zl) * 2 + c)
    right = (dp, lax.rem(x + 1, 4) * 4 + zl * 2 + c)
    left = (dp, lax.rem(x + 3, 4) * 4 + zl * 2 + c)
    above = (lax.rem(y + 1, 4) * 4 + zh, tp)
    below = (lax.rem(y + 3, 4) * 4 + zh, tp)

    load = pltpu.make_async_copy(kvt.at[c], own, load_sem)
    load.start()
    x_loads = []
    for i, src in enumerate((x_own, x1, x2, x3)):
        if i == 0:
            src = src.at[:, pl.ds(pl.multiple_of(x * cols, cols), cols)]
        cp = pltpu.make_async_copy(src, xs.at[lax.rem(x + 4 - i, 4), c], x_sem.at[i])
        cp.start()
        x_loads.append(cp)

    barrier = pltpu.get_barrier_semaphore()
    for partner in (sibling, across, right, left, above, below):
        pl.semaphore_signal(barrier, 1, device_id=partner, device_id_type=MESH)

    def dest(u, q):
        return x * 4 + q, y * 4 + c * 2 + u

    def is_other(d, t):
        return jnp.logical_or(d != dp, t != tp)

    def greet(d, t, n):
        other = is_other(d, t)

        @pl.when(other)
        def _():
            pl.semaphore_signal(barrier, 1, device_id=(d, t), device_id_type=MESH)
        return n + jnp.where(other, 1, 0)

    n = lax.fori_loop(0, 8, lambda i, n: greet(*dest(i // 4, i % 4), n), jnp.int32(6))
    n = lax.fori_loop(0, 8, lambda i, n: greet(x * 4 + i // 2, y * 4 + i % 2 * 2 + zl, n), n)
    pl.semaphore_wait(barrier, n)

    started = []

    def send(src, dst, ss, rs, to):
        cp = pltpu.make_async_remote_copy(src_ref=src, dst_ref=dst, send_sem=ss, recv_sem=rs,
                                          device_id=to, device_id_type=MESH)
        cp.start()
        started.append(cp)
        return cp

    def cut(k):
        return pl.ds(k * rows, rows)

    core = [send(kvt.at[1 - c, :, cut(k)], core_in.at[k], core_s.at[k], core_r.at[k], sibling)
            for k in range(CHUNKS)]
    for cp in x_loads:
        cp.wait()
    x_send = send(xs.at[:, c], xs.at[:, c], xs_s, xs_r, sibling)
    load.wait()

    zc, rc, lc, frc, flc, y1r, y1l, y2r, y2l = ([] for _ in range(9))

    def reduce_core(k):
        core[k].wait_recv()
        part[k] = (own[1 - zl, cut(k)].astype(F32) + core_in[k, 1 - zl].astype(F32)).astype(BF16)
        zc.append(send(part.at[k], z_in.at[k], z_s.at[k], z_r.at[k], across))

    def reduce_z(k):
        zc[k].wait_recv()
        heads[k, x] = (own[zl, cut(k)].astype(F32) + core_in[k, zl].astype(F32) + z_in[k].astype(F32)).astype(BF16)
        here = heads.at[k, x]
        rc.append(send(here, here, right_s.at[k], right_r.at[k], right))
        lc.append(send(here, here, left_s.at[k], left_r.at[k], left))

    def forward(k):
        rc[k].wait_recv()
        a = heads.at[k, lax.rem(x + 3, 4), :, pl.ds(0, half)]
        frc.append(send(a, a, fr_s.at[k], fr_r.at[k], right))
        lc[k].wait_recv()
        b = heads.at[k, lax.rem(x + 1, 4), :, pl.ds(half, half)]
        flc.append(send(b, b, fl_s.at[k], fl_r.at[k], left))

    def multiply(k):
        frc[k].wait_recv()
        flc[k].wait_recv()
        if k == 0:
            x_send.wait_recv()
        lhs = heads[k].reshape(4 * rows, length)
        prod[k] = jnp.dot(lhs, xs[...].reshape(length, cols), preferred_element_type=F32).reshape(4, rows, cols)
        far = prod[k, lax.rem(y + 2, 4)].astype(BF16)
        y1_out[k, 0] = far[:, :mid]
        y1_out[k, 1] = far[:, mid:]
        y1r.append(send(y1_out.at[k, 0], y1_in.at[k, 0], y1r_s.at[k], y1r_r.at[k], above))
        y1l.append(send(y1_out.at[k, 1], y1_in.at[k, 1], y1l_s.at[k], y1l_r.at[k], below))

    def pass_on(k):
        y1r[k].wait_recv()
        mine = prod[k, lax.rem(y + 1, 4)]
        y2_out[k, 0, :, :mid] = (mine[:, :mid] + y1_in[k, 0].astype(F32)).astype(BF16)
        y2_out[k, 0, :, mid:] = mine[:, mid:].astype(BF16)
        y2r.append(send(y2_out.at[k, 0], y2_in.at[k, 0], y2r_s.at[k], y2r_r.at[k], above))
        y1l[k].wait_recv()
        mine = prod[k, lax.rem(y + 3, 4)]
        y2_out[k, 1, :, :mid] = mine[:, :mid].astype(BF16)
        y2_out[k, 1, :, mid:] = (mine[:, mid:] + y1_in[k, 1].astype(F32)).astype(BF16)
        y2l.append(send(y2_out.at[k, 1], y2_in.at[k, 1], y2l_s.at[k], y2l_r.at[k], below))

    spot = zh * 2 + zl

    def out_copy(k, q):
        d, t = dest(k // PARTS, q)
        return d, t, pltpu.make_async_remote_copy(
            src_ref=final.at[k, q], dst_ref=landed.at[spot, k % PARTS], send_sem=out_s.at[k * 4 + q],
            recv_sem=out_r.at[spot, k % PARTS], device_id=(d, t), device_id_type=MESH)

    def deliver(k):
        y2r[k].wait_recv()
        y2l[k].wait_recv()
        total = (prod[k, y] + y2_in[k, 0].astype(F32) + y2_in[k, 1].astype(F32)).astype(BF16)
        for q in range(4):
            final[k, q] = total[:, q * (cols // 4):(q + 1) * (cols // 4)]

        def one(q, carry):
            d, t, cp = out_copy(k, q)
            other = is_other(d, t)

            @pl.when(other)
            def _():
                cp.start()

            @pl.when(jnp.logical_not(other))
            def _():
                pltpu.make_async_copy(final.at[k, q], landed.at[spot, k % PARTS], out_r.at[spot, k % PARTS]).start()
            return carry
        lax.fori_loop(0, 4, one, 0)

    stages = (reduce_core, reduce_z, forward, multiply, pass_on, deliver)
    for step in range(CHUNKS + len(stages) - 1):
        for i, stage in enumerate(stages):
            if 0 <= step - i < CHUNKS:
                stage(step - i)

    def collect(i, total):
        new = []
        for p in range(PARTS):
            pltpu.make_async_copy(landed.at[i, p], landed.at[i, p], out_r.at[i, p]).wait()
            new.append(total[p] + landed[i, p].astype(F32))
        return tuple(new)

    zero = jnp.zeros((rows, cols // 4), F32)
    sums = lax.fori_loop(0, 8, collect, (zero,) * PARTS)
    for p in range(PARTS):
        out_ref[p * rows:(p + 1) * rows] = sums[p]

    for cp in started:
        cp.wait_send()

    def drain(j, carry):
        d, t, cp = out_copy(j // 4, j % 4)

        @pl.when(is_other(d, t))
        def _():
            cp.wait_send()
        return carry
    lax.fori_loop(0, 4 * CHUNKS, drain, 0)


def exchange(kvt, x_own, others):
    length = kvt.shape[3]
    cols = others[0].shape[1]
    rows = HD // CHUNKS
    sem = pltpu.SemaphoreType.DMA
    n = CHUNKS
    return pl.pallas_call(
        exchange_kernel,
        out_shape=jax.ShapeDtypeStruct((PARTS * rows, cols // 4), F32),
        in_specs=[pl.BlockSpec(memory_space=pl.ANY)] * 5,
        out_specs=pl.BlockSpec(memory_space=pltpu.VMEM),
        scratch_shapes=[
            pltpu.VMEM((2, HD, length), BF16), pltpu.VMEM((n, 2, rows, length), BF16),
            pltpu.VMEM((n, rows, length), BF16), pltpu.VMEM((n, rows, length), BF16),
            pltpu.VMEM((n, 4, rows, length), BF16), pltpu.VMEM((4, 2, TILE, cols), BF16),
            pltpu.VMEM((n, 4, rows, cols), F32),
            pltpu.VMEM((n, 2, rows, cols // 2), BF16), pltpu.VMEM((n, 2, rows, cols // 2), BF16),
            pltpu.VMEM((n, 2, rows, cols), BF16), pltpu.VMEM((n, 2, rows, cols), BF16),
            pltpu.VMEM((n, 4, rows, cols // 4), BF16), pltpu.VMEM((8, PARTS, rows, cols // 4), BF16),
        ] + [sem((n,))] * 20 + [sem, sem, sem, sem((4,)), sem((4 * n,)), sem((8, PARTS))],
        compiler_params=pltpu.CompilerParams(collective_id=0, has_side_effects=True, vmem_limit_bytes=56 << 20),
        cost_estimate=pl.CostEstimate(flops=10**9, bytes_accessed=8 << 20, transcendentals=0),
        name="exchange",
    )(kvt, x_own, *others)


def local(input_rows, queries, key_values, out_grad, item_logratio, pair_ids, tile_item, tile_image):
    t = lax.axis_index("tp")
    rows = input_rows[0]
    cols = rows.shape[1] // 4
    others = []
    for dx in range(1, 4):
        to = (t // 4 + dx) % 4
        pairs = [(a, (a + 4 * dx) % 16) for a in range(16)]
        others.append(lax.ppermute(lax.dynamic_slice_in_dim(rows, to * cols, cols, 1), "tp", pairs))
    dq, kvt = attention(queries, out_grad, key_values, item_logratio, pair_ids, tile_item, tile_image)
    return dq, exchange(kvt, rows, others).T


def solution(mesh):
    in_specs = (P("dp", "tp", None), P("dp", None, "tp"), P("dp", None, None), P("dp", None, "tp"),
                P("dp", None), P("dp", None), P("dp", None), P("dp", None))
    out_specs = (P("dp", None, "tp"), P("dp", "tp"))
    return jax.shard_map(local, mesh=mesh, in_specs=in_specs, out_specs=out_specs, check_vma=False)
```

time: 209 us -> 81.3 us (0.39)
  the two profiles are of different devices: /device:TPU:36 before, /device:TPU:15 now
where the time goes in v3:
time: 81.3 us; the launch traced here: 81.1 us
  Pallas kernels  74 us (91%)
  local copies, waits for them, and re-layouts  3.51 us (4%)
  starting transfers between devices  2.76 us (3%)
    pallas_call x1, Pallas kernels, exchange(): pl.pallas_call(exchange_kernel, out_shape=jax.ShapeDtypeStruct((PARTS * r...  59.7 us
    pallas_call x1, Pallas kernels, attention(): pl.pallas_call(attention_kernel, out_shape=[jax.ShapeDtypeStruct(queries....  14.4 us
    ppermute x3, starting transfers between devices, local(): lax.ppermute(lax.dynamic_slice_in_dim(rows, to * cols, cols, 1), 'tp', pa...  2.76 us
    unnamed x7, local copies, waits for them, and re-layouts  2.34 us
  transfers between devices with their start and end apart: 3, of which 0 were waited for; matrix products, arithmetic and copies ran while one was open for 0% of the time, Pallas kernels for 18%

profile of v3, /device:TPU:15, one launch (start us, length us, event | category | flops | bytes accessed | tf_op | source)
XLA Modules:
  0.0 81.1 jit_solution(12049713047821719304)
XLA Ops:
  0.7 1.2 %dynamic-slice_bitcast_fusion = (bf16[128,1024]{1,0:T(8,128)(2,1)S(1)}, bf16[128,1024]{1,0:T(8,128)(2,1)S(1)}, bf16[128,1024]{1,0:T(8,128)(2,1)S(1)}) fusion(bf16[1,128,4096]{2,1,0:T(8,128)(2,1)} %param.8, s32[]{:T(128)S(6)} %select_n.36, s32[]{:T(128)S(6)} %select_n.32, s32[]{:T(128)S(6)} %select_n.34), kind=kLoop, calls=%fused_computation | loop fusion | bytes 1572876 | tf_op jit(solution)/shard_map/dynamic_slice | solution.py:428
  1.9 0.6 collective-permute-start.2
  2.5 2.1 %collective-permute-start = (bf16[128,1024]{1,0:T(8,128)(2,1)S(1)}, bf16[128,1024]{1,0:T(8,128)(2,1)S(1)}, u32[]{:S(2)}, u32[]{:S(2)}) collective-permute-start(bf16[128,1024]{1,0:T(8,128)(2,1)S(1)} %get-tuple-element.7), channel_id=1, source_target_pairs={{0,4},{1,5},{2,6},{3,7},{4,8},{5,9},{6,10},{7,11},{8,12},{9,13},{1... | collective-permute-start | bytes 786440 | tf_op jit(solution)/shard_map/ppermute | solution.py:428
  4.6 0.0 collective-permute-start.1
  4.6 14.4 %attention.1 = (bf16[1,2048,256]{2,1,0:T(8,128)(2,1)}, bf16[2,2,128,1024]{3,2,1,0:T(8,128)(2,1)}) custom-call(f32[1,4]{1,0:T(1,128)} %ratio_h.1, s32[1,4]{1,0:T(1,128)} %pair_h.1, s32[1,16]{1,0:T(1,128)} %item_h.1, s32[1,16]{1,0:T(1,128)} %image_h.1, bf16[1,2048,256]{2,1,0:T(8,128)(2,1)} %q_hbm.1, bf16[1,2048,256]{2,1,0:T(8,128)(2,1)} %og_hbm.1, ...), custom_call_target="tpu_custom_call" | custom-call | flops 10000000000 | bytes 8388608 | tf_op jit(solution)/shard_map/attention/pallas_call | solution.py:183
  19.0 0.0 collective-permute-done.2.x3
  19.0 0.0 copy-start
  19.0 0.0 collective-permute-done.x1
  19.0 0.0 copy-start.1
  19.1 0.0 collective-permute-done.1.x2
  19.1 0.0 copy-start.2
  19.1 0.6 copy-done
  19.7 0.1 copy-done.1
  19.8 0.1 copy-done.2
  19.9 59.7 %exchange.1 = f32[64,256]{1,0:T(8,128)} custom-call(bf16[2,2,128,1024]{3,2,1,0:T(8,128)(2,1)} %get-tuple-element.5.kvt, bf16[128,4096]{1,0:T(8,128)(2,1)} %bitcast.8, bf16[128,1024]{1,0:T(8,128)(2,1)} %copy-done.1, bf16[128,1024]{1,0:T(8,128)(2,1)} %copy-done.2, bf16[128,1024]{1,0:T(8,128)(2,1)} %copy-done), custom_call_target="tpu_custom_call" | custom-call | flops 1000000000 | bytes 8388608 | tf_op jit(solution)/shard_map/exchange/pallas_call | solution.py:400
  79.6 1.5 %copy.11 = f32[256,64]{0,1:T(8,128)} copy(f32[256,64]{0,1:T(8,128)} %bitcast.9) | data formatting | bytes 131072
Async XLA Ops:
  1.9 17.1 %collective-permute-start.2 = (bf16[128,1024]{1,0:T(8,128)(2,1)S(1)}, bf16[128,1024]{1,0:T(8,128)(2,1)S(1)}, u32[]{:S(2)}, u32[]{:S(2)}) collective-permute-start(bf16[128,1024]{1,0:T(8,128)(2,1)S(1)} %get-tuple-element.6), channel_id=1, source_target_pairs={{0,12},{1,13},{2,14},{3,15},{4,0},{5,1},{6,2},{7,3},{8,4},{9,5},{1... | collective-permute-start | bytes 786440 | tf_op jit(solution)/shard_map/ppermute | solution.py:428
  2.5 16.5 %collective-permute-start = (bf16[128,1024]{1,0:T(8,128)(2,1)S(1)}, bf16[128,1024]{1,0:T(8,128)(2,1)S(1)}, u32[]{:S(2)}, u32[]{:S(2)}) collective-permute-start(bf16[128,1024]{1,0:T(8,128)(2,1)S(1)} %get-tuple-element.7), channel_id=1, source_target_pairs={{0,4},{1,5},{2,6},{3,7},{4,8},{5,9},{6,10},{7,11},{8,12},{9,13},{1... | collective-permute-start | bytes 786440 | tf_op jit(solution)/shard_map/ppermute | solution.py:428
  4.6 14.4 %collective-permute-start.1 = (bf16[128,1024]{1,0:T(8,128)(2,1)S(1)}, bf16[128,1024]{1,0:T(8,128)(2,1)S(1)}, u32[]{:S(2)}, u32[]{:S(2)}) collective-permute-start(bf16[128,1024]{1,0:T(8,128)(2,1)S(1)} %get-tuple-element.8), channel_id=1, source_target_pairs={{0,8},{1,9},{2,10},{3,11},{4,12},{5,13},{6,14},{7,15},{8,0},{9,1},... | collective-permute-start | bytes 786440 | tf_op jit(solution)/shard_map/ppermute | solution.py:428
  19.0 0.7 copy-start
  19.0 0.8 copy-start.1
  19.1 0.9 %copy-start.2 = (bf16[128,1024]{1,0:T(8,128)(2,1)}, bf16[128,1024]{1,0:T(8,128)(2,1)S(1)}, u32[]{:S(2)}) copy-start(bf16[128,1024]{1,0:T(8,128)(2,1)S(1)} %collective-permute-done.1.x2) | copy-start | bytes 786436
